TPU v7x, 256 devices: a whole 4x4x8 slice. The times are simulated.
256 devices in a mesh: grp: 4 (over z_hi, core), gx: 16 (over x, z_lo), gy: 4 (over y).
Axes of the slice: x: 4, y: 4, z: 8 (z_hi: 2, z_lo: 4; z = z_hi * 4 + z_lo), core: 2. Of those that a mesh axis runs over, the one named last changes fastest.
Arguments:
- wind_u: float32 [32, 1024, 1024], P('gx', 'grp', 'gy'), may hold values from -0.25 to 0.25
- wind_v: float32 [32, 1024, 1024], P('gx', 'grp', 'gy'), may hold values from -0.25 to 0.25
- theta: float32 [32, 1024, 1024], P('gx', 'grp', 'gy'), may hold values from 0.8 to 1.2
- ash: float32 [8, 32, 1024, 1024], P(None, None, ('grp', 'gx'), 'gy'), may hold values from 0.05 to 2
- src_x: int32 [16], replicated, may hold values from 0 to 1023
- src_y: int32 [16], replicated, may hold values from 0 to 1023
- src_rate: float32 [16, 8, 32], replicated, may hold values from 0.1 to 1
- settle_class: int32 [8], replicated, may hold values from 0 to 3
- settle_table: float32 [4], replicated, may hold values from 0.01 to 0.05
Outputs:
- ash_next: float32 [8, 32, 1024, 1024], P(None, None, ('grp', 'gx'), 'gy')
- met_next: float32 [3, 32, 1024, 1024], P(None, 'gx', 'grp', 'gy')
All inputs are finite; a program needn't handle non-finite values.
Results may differ from a plain program's by a relative error of at most 0.00005.
Values sent between devices are 32-bit elements; how exact they have to be, the bound alone decides.
A program may use at most 128 MiB of HBM per device.

v0:
```python
import jax
import jax.numpy as jnp
from jax import lax
from jax.sharding import PartitionSpec as P

diffuse_rate = 0.1
lift_scale = 0.1
lift_limit = 0.15
eddy_base = 0.005
eddy_slope = 0.03
mixing_base = 0.005
mixing_slope = 0.08
stable_weight = 20.0
level_decay = 32.0


def extended(array, sides, width):
    for axis, dim in sides:
        peers, length = (lax.axis_size(axis), array.shape[dim])
        up = [(i, (i + 1) % peers) for i in range(peers - 1)]
        down = [(j, i) for i, j in up]
        last = lax.slice_in_dim(array, length - width, length, axis=dim)
        initial = lax.slice_in_dim(array, 0, width, axis=dim)
        before = lax.ppermute(last, axis, up)
        after = lax.ppermute(initial, axis, down)
        array = jnp.concatenate([before, array, after], axis=dim)
    return array


def entering(part, axis, combine, identity):
    place = lax.axis_index(axis)
    gathered = lax.all_gather(part, axis)
    state = jnp.zeros_like(part) + jnp.asarray(identity, part.dtype)

    def one(step, state):
        return combine(state, lax.dynamic_index_in_dim(gathered, step, 0, False))

    return lax.fori_loop(0, place, one, state)


def sides(padded):
    return (
        padded[..., 2:, 1:-1],
        padded[..., :-2, 1:-1],
        padded[..., 1:-1, 2:],
        padded[..., 1:-1, :-2],
    )


def vertical_sides(field, axis):
    count = field.shape[axis]
    upper = jnp.concatenate(
        [
            lax.slice_in_dim(field, 1, count, axis=axis),
            lax.slice_in_dim(field, count - 1, count, axis=axis),
        ],
        axis,
    )
    lower = jnp.concatenate(
        [
            lax.slice_in_dim(field, 0, 1, axis=axis),
            lax.slice_in_dim(field, 0, count - 1, axis=axis),
        ],
        axis,
    )
    return (upper, lower)


def horizontal(padded_zonal, padded_merid):
    zonal_east, zonal_west, zonal_north, zonal_south = sides(padded_zonal)
    merid_east, merid_west, merid_north, merid_south = sides(padded_merid)
    xstretch = 0.5 * (zonal_east - zonal_west)
    yshear = 0.5 * (zonal_north - zonal_south)
    xshear = 0.5 * (merid_east - merid_west)
    ystretch = 0.5 * (merid_north - merid_south)
    divergence = xstretch + ystretch
    eddy = eddy_base + eddy_slope * jnp.sqrt((xstretch - ystretch) ** 2 + (yshear + xshear) ** 2)
    return (divergence, eddy)


def mixing_of(zonal_slope, merid_slope, warm_slope):
    return mixing_base + mixing_slope * jnp.sqrt(zonal_slope**2 + merid_slope**2) / (
        1.0 + stable_weight * jnp.maximum(warm_slope, 0.0)
    )


def transport(conc, rim, zonal, merid, lifted, eddy, mixing, settling):
    east, west, north, south = sides(rim)
    upper, lower = vertical_sides(conc, 1)
    advect = jnp.maximum(zonal, 0.0) * (conc - west) + jnp.minimum(zonal, 0.0) * (east - conc)
    advect = (
        advect + jnp.maximum(merid, 0.0) * (conc - south) + jnp.minimum(merid, 0.0) * (north - conc)
    )
    advect = (
        advect
        + jnp.maximum(lifted, 0.0) * (conc - lower)
        + jnp.minimum(lifted, 0.0) * (upper - conc)
    )
    spread = eddy * (east + west + north + south - 4.0 * conc) + mixing * (
        upper - 2.0 * conc + lower
    )
    flux = settling * conc
    flux_above = jnp.concatenate([flux[:, 1:], jnp.zeros_like(flux[:, :1])], axis=1)
    return conc - advect + spread + flux_above - flux


def body(wind_u, wind_v, theta, ash, src_x, src_y, src_rate, settle_class, settle_table):
    levels = wind_u.shape[0]
    state = jnp.stack([wind_u, wind_v, theta])
    padded = extended(state, (("grp", 2), ("gx", 1), ("gy", 3)), 1)
    level_index = lax.axis_index("gx")
    last_index = lax.axis_size("gx") - 1
    flat = padded[:, :, 1:-1, 1:-1]
    beneath = jnp.where(level_index == 0, state[:, :1], flat[:, :1])
    overhead = jnp.where(level_index == last_index, state[:, -1:], flat[:, -1:])
    upper = jnp.concatenate([flat[:, 2:-1], overhead], axis=1)
    lower = jnp.concatenate([beneath, flat[:, 1:-2]], axis=1)
    slopes = 0.5 * (upper - lower)
    horiz = padded[:, 1:-1]
    divergence, eddy = horizontal(horiz[0], horiz[1])
    column = jnp.sum(divergence, axis=0)
    prefix = entering(column, "gx", lambda early, later: early + later, jnp.zeros_like(column))
    lifted = jnp.clip(
        -lift_scale * (prefix[None] + jnp.cumsum(divergence, axis=0)), -lift_limit, lift_limit
    )
    east, west, north, south = sides(horiz)
    laplace = east + west + north + south - 4.0 * state
    met_next = jnp.stack(
        [
            wind_u + diffuse_rate * laplace[0] - lifted * slopes[0],
            wind_v + diffuse_rate * laplace[1] - lifted * slopes[1],
            theta - lifted * slopes[2],
        ]
    )
    tiles = lax.axis_size("gx")
    start_x = (lax.axis_index("grp") * tiles + lax.axis_index("gx")) * ash.shape[2]
    start_y = lax.axis_index("gy") * ash.shape[3]
    xpick = (src_x[:, None] - start_x == jnp.arange(ash.shape[2], dtype=jnp.int32)[None]).astype(
        jnp.float32
    )
    ypick = (src_y[:, None] - start_y == jnp.arange(ash.shape[3], dtype=jnp.int32)[None]).astype(
        jnp.float32
    )
    emission = jnp.einsum(
        "sbk,si,sj->bkij", src_rate, xpick, ypick, precision=lax.Precision.HIGHEST
    )
    conc = ash + emission
    classes = (
        settle_class[:, None] == jnp.arange(settle_table.shape[0], dtype=jnp.int32)[None]
    ).astype(jnp.float32)
    speeds = jnp.dot(classes, settle_table, precision=lax.Precision.HIGHEST)
    level = (level_index * levels + jnp.arange(levels, dtype=jnp.int32)).astype(jnp.float32)
    mixing = mixing_of(slopes[0], slopes[1], slopes[2])
    density = jnp.sqrt(theta) * jnp.exp(level / level_decay)[:, None, None]
    moved = lax.all_to_all(
        jnp.stack([wind_u, wind_v, lifted, eddy, mixing, density]),
        "gx",
        split_axis=2,
        concat_axis=1,
        tiled=True,
    )
    rim = extended(conc, ((("grp", "gx"), 2), ("gy", 3)), 1)
    zonal, merid, column_lift, column_eddy, column_mixing, column_density = (
        moved[0],
        moved[1],
        moved[2],
        moved[3],
        moved[4],
        moved[5],
    )
    settling = speeds[:, None, None, None] * column_density[None]
    ash_next = transport(conc, rim, zonal, merid, column_lift, column_eddy, column_mixing, settling)
    return (ash_next, met_next)


def solution(mesh):
    in_specs = (
        P("gx", "grp", "gy"),
        P("gx", "grp", "gy"),
        P("gx", "grp", "gy"),
        P(None, None, ("grp", "gx"), "gy"),
        P(),
        P(),
        P(),
        P(),
        P(),
    )
    out_specs = (P(None, None, ("grp", "gx"), "gy"), P(None, "gx", "grp", "gy"))
    return jax.shard_map(body, mesh=mesh, in_specs=in_specs, out_specs=out_specs, check_vma=False)
```

profile of v0, /device:TPU:1, one launch (start us, length us, event | category | flops | bytes accessed | tf_op | source)
XLA Modules:
  0.0 379.9 jit_solution(15452553302783704308)
XLA Ops:
  8.9 10.2 %collective-permute-start = (f32[3,2,1,256]{3,2,1,0:T(1,128)S(1)}, f32[3,2,1,256]{3,2,1,0:T(1,128)S(1)}, u32[]{:S(2)}, u32[]{:S(2)}) collective-permute-start(f32[3,2,1,256]{3,2,1,0:T(1,128)S(1)} %get-tuple-element.72), channel_id=1, source_target_pairs={{0,64},{64,128},{128,192},{1,65},{65,129},{129,193},{2,66},{66,130... | collective-permute-start | bytes 18440 | tf_op jit(solution)/shard_map/ppermute | solution.py:24
  21.0 6.9 %collective-permute-done.1 = f32[3,2,1,256]{3,2,1,0:T(1,128)S(1)} collective-permute-done((f32[3,2,1,256]{3,2,1,0:T(1,128)S(1)}, f32[3,2,1,256]{3,2,1,0:T(1,128)S(1)}, u32[]{:S(2)}, u32[]{:S(2)}) %collective-permute-start.1) | collective-permute-done | bytes 6176 | tf_op jit(solution)/shard_map/ppermute | solution.py:25
  31.2 4.0 %collective-permute-start.2 = (f32[3,1,258,256]{3,1,2,0:T(1,128)S(1)}, f32[3,1,258,256]{3,1,2,0:T(1,128)S(1)}, u32[]{:S(2)}, u32[]{:S(2)}) collective-permute-start(f32[3,1,258,256]{3,1,2,0:T(1,128)S(1)} %copy.85), channel_id=1, source_target_pairs={{0,4},{4,8},{8,12},{12,16},{16,20},{20,24},{24,28},{28,32},{32,36}... | collective-permute-start | bytes 2377736 | tf_op jit(solution)/shard_map/ppermute | solution.py:24
  35.2 14.3 %collective-permute-done.3 = f32[3,1,258,256]{3,1,2,0:T(1,128)S(1)} collective-permute-done((f32[3,1,258,256]{3,1,2,0:T(1,128)S(1)}, f32[3,1,258,256]{3,1,2,0:T(1,128)S(1)}, u32[]{:S(2)}, u32[]{:S(2)}) %collective-permute-start.3) | collective-permute-done | bytes 792608 | tf_op jit(solution)/shard_map/ppermute | solution.py:25
  54.3 3.2 collective-permute-start.4
  66.0 5.8 %pad_maximum_fusion = f32[3,4,258,258]{3,2,1,0:T(8,128)S(1)} fusion(f32[3,4,258,1]{3,2,1,0:T(8,128)} %copy.92, f32[3,1,258,256]{3,2,1,0:T(8,128)S(1)} %copy.88, f32[3,2,1,256]{3,2,1,0:T(1,128)S(1)} %collective-permute-done.1, f32[1,2,256,256]{3,2,1,0:T(8,128)S(1)} %bitcast.104, f32[1,2,256,256]{3,2,1,0:T(8,128)S(1)} %bitcast.99, ...), kind=kLoop, calls=%fused_computation.1 | loop fusion | flops 6390144 | bytes 6390144 | tf_op jit(solution)/shard_map/concatenate | solution.py:26
  78.4 109.6 %all-gather.3.cloned.1.call-done = f32[4096,256]{1,0:T(8,128)} async-done(((f32[256,256]{1,0:T(8,128)}), f32[4096,256]{1,0:T(8,128)}) %all-gather.3.cloned.1.call-update) | async-done | bytes 4194320 | tf_op jit(solution)/shard_map/all_gather | solution.py:32
  193.4 6.0 %copy.95 = f32[6,2,256,256]{3,1,0,2:T(2,128)} copy(f32[6,2,256,256]{3,2,1,0:T(8,128)} %bitcast_dynamic-update-slice_fusion) | data formatting | bytes 6291456 | tf_op jit(solution)/shard_map/stack | solution.py:156
  199.4 19.2 %all-to-all-start = ((f32[6,2,256,256]{3,1,0,2:T(2,128)}), f32[6,2,256,256]{3,1,0,2:T(2,128)}, u32[]{:S(2)}, u32[]{:S(2)}) async-start(f32[6,2,256,256]{3,1,0,2:T(2,128)} %copy.95), calls=%async_computation | async-start | bytes 6291456 | tf_op jit(solution)/shard_map/all_to_all | solution.py:155
  220.4 5.1 %fusion.27 = f32[3,2,256,256]{3,2,1,0:T(8,128)S(1)} fusion(f32[1,2,256,256]{3,2,1,0:T(8,128)S(1)} %bitcast.95, f32[1,2,256,256]{3,2,1,0:T(8,128)S(1)} %bitcast.100, f32[3,4,258,1]{3,2,1,0:T(8,128)} %copy.91, f32[3,1,258,256]{3,2,1,0:T(8,128)S(1)} %copy-done.7, f32[3,1,258,256]{3,2,1,0:T(8,128)S(1)} %copy-done.9, ...), kind=kLoop, calls=%fused_computation.49 | loop fusion | flops 10616832 | bytes 4767936 | tf_op jit(solution)/shard_map/sub | solution.py:127
  227.1 63.8 %all-to-all-done = f32[6,2,256,256]{3,1,0,2:T(2,128)} async-done(((f32[6,2,256,256]{3,1,0,2:T(2,128)}), f32[6,2,256,256]{3,1,0,2:T(2,128)}, u32[]{:S(2)}, u32[]{:S(2)}) %all-to-all-start) | async-done | bytes 3145760 | tf_op jit(solution)/shard_map/all_to_all | solution.py:155
  296.4 5.7 %multiply_multiply_fusion = (f32[8,32,16,256]{3,1,0,2:T(8,128)}, f32[8,32,16,256]{3,1,0,2:T(8,128)S(1)}) fusion(f32[32,16,256]{2,0,1:T(8,128)S(1)} %copy.110, f32[8]{0:T(128)S(1)} %convolution_bitcast_fusion, s32[16]{0:T(128)S(1)} %broadcast_subtract_fusion, f32[16,8,32]{2,0,1:T(8,128)S(1)} %copy.83, f32[16,16]{0,1:T(8,128)S(1)} %fusion.70, ...), kind=kOutput, calls=%fused_computation.37 | convolution fusion | flops 204541952 | bytes 13124704 | tf_op jit(solution)/shard_map/sbk,si,sj->bkij/dot_general | solution.py:144
  304.0 7.8 %collective-permute-start.7 = (f32[8,32,1,256]{3,1,0,2:T(8,128)S(1)}, f32[8,32,1,256]{3,1,0,2:T(8,128)S(1)}, u32[]{:S(2)}, u32[]{:S(2)}) collective-permute-start(f32[8,32,1,256]{3,1,0,2:T(8,128)S(1)} %get-tuple-element.51), channel_id=1, source_target_pairs={{4,0},{8,4},{12,8},{16,12},{20,16},{24,20},{28,24},{32,28},{36,32}... | collective-permute-start | bytes 786440 | tf_op jit(solution)/shard_map/ppermute | solution.py:25
  311.8 4.4 %fusion.77 = (f32[8,31,16,256]{3,1,0,2:T(8,128)}, f32[8,31,16,256]{3,1,0,2:T(8,128)}) fusion(f32[8,32,16,256]{3,1,0,2:T(8,128)S(1)} %get-tuple-element.77), kind=kLoop, calls=%fused_computation.138 | loop fusion | bytes 16252928 | tf_op jit(solution)/shard_map/slice | solution.py:62
  316.2 3.0 collective-permute-done.7
  320.0 3.0 fusion.75
  323.0 3.2 copy.101
  326.2 3.2 copy.104
  330.8 4.6 %collective-permute-start.8 = (f32[8,32,18,1]{1,0,3,2:T(8,128)}, f32[8,32,18,1]{1,0,3,2:T(8,128)}, u32[]{:S(2)}, u32[]{:S(2)}) collective-permute-start(f32[8,32,18,1]{1,0,3,2:T(8,128)} %copy.101), channel_id=1, source_target_pairs={{0,1},{1,2},{2,3},{4,5},{5,6},{6,7},{8,9},{9,10},{10,11},{12,13},{... | collective-permute-start | bytes 55304 | tf_op jit(solution)/shard_map/ppermute | solution.py:24
  342.8 2.6 slice.270
  345.4 3.2 copy.102
  348.6 3.2 copy.105
  351.8 16.8 %fusion.9 = f32[8,32,16,256]{3,1,0,2:T(8,128)S(1)} fusion(f32[8,32,1,256]{3,1,0,2:T(8,128)} %copy-done.20, f32[8,32,16,256]{3,1,0,2:T(8,128)} %copy-done.2, f32[8,32,1,256]{3,1,0,2:T(8,128)S(1)} %collective-permute-done.6, f32[8,31,16,256]{3,1,0,2:T(8,128)} %slice.270, f32[8,1,16,256]{3,1,0,2:T(1,128)} %get-tuple-element.47, ...), kind=kLoop, calls=%fused_computation.23 | loop fusion | flops 46137344 | bytes 26120224 | tf_op jit(solution)/shard_map/sub | solution.py:104
  368.6 4.4 %copy.113 = f32[8,32,16,256]{3,2,1,0:T(8,128)} copy(f32[8,32,16,256]{3,1,0,2:T(8,128)S(1)} %fusion.9) | data formatting | bytes 8388608
  (108 shorter events, 52.1 us)
Async XLA Ops:
  7.2 212.3 %copy-start = (f32[4]{0:T(128)S(1)}, f32[4]{0:T(128)}, u32[]{:S(2)}) copy-start(f32[4]{0:T(128)} %param.19) | copy-start | bytes 52
  7.2 20.7 %copy-start.5 = (f32[2,256,256]{2,1,0:T(8,128)S(1)}, f32[2,256,256]{2,1,0:T(8,128)}, u32[]{:S(2)}) copy-start(f32[2,256,256]{2,1,0:T(8,128)} %param.13) | copy-start | bytes 1572868
  7.2 20.7 %copy-start.4 = (f32[2,256,256]{2,1,0:T(8,128)S(1)}, f32[2,256,256]{2,1,0:T(8,128)}, u32[]{:S(2)}) copy-start(f32[2,256,256]{2,1,0:T(8,128)} %param.12) | copy-start | bytes 1572868
  7.2 20.7 %copy-start.3 = (f32[2,256,256]{2,1,0:T(8,128)S(1)}, f32[2,256,256]{2,1,0:T(8,128)}, u32[]{:S(2)}) copy-start(f32[2,256,256]{2,1,0:T(8,128)} %param.11) | copy-start | bytes 1572868
  7.2 180.7 %all-gather.3.cloned.1.call-start = ((), (), s32[]{:S(2)}) async-start(), calls=%async_computation.1 | async-start | bytes 4456448 | tf_op jit(solution)/shard_map/all_gather | solution.py:32
  8.9 12.1 %collective-permute-start = (f32[3,2,1,256]{3,2,1,0:T(1,128)S(1)}, f32[3,2,1,256]{3,2,1,0:T(1,128)S(1)}, u32[]{:S(2)}, u32[]{:S(2)}) collective-permute-start(f32[3,2,1,256]{3,2,1,0:T(1,128)S(1)} %get-tuple-element.72), channel_id=1, source_target_pairs={{0,64},{64,128},{128,192},{1,65},{65,129},{129,193},{2,66},{66,130... | collective-permute-start | bytes 18440 | tf_op jit(solution)/shard_map/ppermute | solution.py:24
  19.1 8.9 %collective-permute-start.1 = (f32[3,2,1,256]{3,2,1,0:T(1,128)S(1)}, f32[3,2,1,256]{3,2,1,0:T(1,128)S(1)}, u32[]{:S(2)}, u32[]{:S(2)}) collective-permute-start(f32[3,2,1,256]{3,2,1,0:T(1,128)S(1)} %get-tuple-element.73), channel_id=1, source_target_pairs={{64,0},{128,64},{192,128},{65,1},{129,65},{193,129},{66,2},{130,66... | collective-permute-start | bytes 18440 | tf_op jit(solution)/shard_map/ppermute | solution.py:25
  29.0 20.4 %collective-permute-start.3 = (f32[3,1,258,256]{3,1,2,0:T(1,128)S(1)}, f32[3,1,258,256]{3,1,2,0:T(1,128)S(1)}, u32[]{:S(2)}, u32[]{:S(2)}) collective-permute-start(f32[3,1,258,256]{3,1,2,0:T(1,128)S(1)} %copy.86), channel_id=1, source_target_pairs={{4,0},{8,4},{12,8},{16,12},{20,16},{24,20},{28,24},{32,28},{36,32}... | collective-permute-start | bytes 2377736 | tf_op jit(solution)/shard_map/ppermute | solution.py:25
  31.2 18.4 %collective-permute-start.2 = (f32[3,1,258,256]{3,1,2,0:T(1,128)S(1)}, f32[3,1,258,256]{3,1,2,0:T(1,128)S(1)}, u32[]{:S(2)}, u32[]{:S(2)}) collective-permute-start(f32[3,1,258,256]{3,1,2,0:T(1,128)S(1)} %copy.85), channel_id=1, source_target_pairs={{0,4},{4,8},{8,12},{12,16},{16,20},{20,24},{24,28},{28,32},{32,36}... | collective-permute-start | bytes 2377736 | tf_op jit(solution)/shard_map/ppermute | solution.py:24
  49.5 16.4 %copy-start.6 = (f32[3,1,258,256]{3,2,1,0:T(8,128)}, f32[3,1,258,256]{3,2,1,0:T(8,128)S(1)}, u32[]{:S(2)}) copy-start(f32[3,1,258,256]{3,2,1,0:T(8,128)S(1)} %copy.88) | copy-start | bytes 2377732
  49.6 16.3 %copy-start.8 = (f32[3,1,258,256]{3,2,1,0:T(8,128)}, f32[3,1,258,256]{3,2,1,0:T(8,128)S(1)}, u32[]{:S(2)}) copy-start(f32[3,1,258,256]{3,2,1,0:T(8,128)S(1)} %copy.87) | copy-start | bytes 2377732
  54.3 6.6 %collective-permute-start.4 = (f32[3,4,258,1]{2,1,3,0:T(4,128)S(1)}, f32[3,4,258,1]{2,1,3,0:T(4,128)S(1)}, u32[]{:S(2)}, u32[]{:S(2)}) collective-permute-start(f32[3,4,258,1]{2,1,3,0:T(4,128)S(1)} %copy.89), channel_id=1, source_target_pairs={{0,1},{1,2},{2,3},{4,5},{5,6},{6,7},{8,9},{9,10},{10,11},{12,13},{... | collective-permute-start | bytes 37160 | tf_op jit(solution)/shard_map/ppermute | solution.py:24
  59.7 4.5 %collective-permute-start.5 = (f32[3,4,258,1]{2,1,3,0:T(4,128)S(1)}, f32[3,4,258,1]{2,1,3,0:T(4,128)S(1)}, u32[]{:S(2)}, u32[]{:S(2)}) collective-permute-start(f32[3,4,258,1]{2,1,3,0:T(4,128)S(1)} %copy.90), channel_id=1, source_target_pairs={{1,0},{2,1},{3,2},{5,4},{6,5},{7,6},{9,8},{10,9},{11,10},{13,12},{... | collective-permute-start | bytes 37160 | tf_op jit(solution)/shard_map/ppermute | solution.py:25
  199.4 20.1 %copy-start.21 = (s32[8]{0:T(128)S(1)}, s32[8]{0:T(128)}, u32[]{:S(2)}) copy-start(s32[8]{0:T(128)} %param.18) | copy-start | bytes 100
  199.4 20.3 %copy-start.22 = (s32[16]{0:T(128)S(1)}, s32[16]{0:T(128)}, u32[]{:S(2)}) copy-start(s32[16]{0:T(128)} %param.16) | copy-start | bytes 196
  199.4 21.0 %copy-start.7 = (f32[3,1,258,256]{3,2,1,0:T(8,128)S(1)}, f32[3,1,258,256]{3,2,1,0:T(8,128)}, u32[]{:S(2)}) copy-start(f32[3,1,258,256]{3,2,1,0:T(8,128)} %copy-done.6) | copy-start | bytes 2377732
  199.4 21.0 %copy-start.9 = (f32[3,1,258,256]{3,2,1,0:T(8,128)S(1)}, f32[3,1,258,256]{3,2,1,0:T(8,128)}, u32[]{:S(2)}) copy-start(f32[3,1,258,256]{3,2,1,0:T(8,128)} %copy-done.8) | copy-start | bytes 2377732
  199.4 91.5 %all-to-all-start = ((f32[6,2,256,256]{3,1,0,2:T(2,128)}), f32[6,2,256,256]{3,1,0,2:T(2,128)}, u32[]{:S(2)}, u32[]{:S(2)}) async-start(f32[6,2,256,256]{3,1,0,2:T(2,128)} %copy.95), calls=%async_computation | async-start | bytes 6291456 | tf_op jit(solution)/shard_map/all_to_all | solution.py:155
  302.1 17.2 %copy-start.2 = (f32[8,32,16,256]{3,1,0,2:T(8,128)}, f32[8,32,16,256]{3,1,0,2:T(8,128)S(1)}, u32[]{:S(2)}) copy-start(f32[8,32,16,256]{3,1,0,2:T(8,128)S(1)} %get-tuple-element.77) | copy-start | bytes 12582916
  302.1 14.1 %collective-permute-start.6 = (f32[8,32,1,256]{3,1,0,2:T(8,128)S(1)}, f32[8,32,1,256]{3,1,0,2:T(8,128)S(1)}, u32[]{:S(2)}, u32[]{:S(2)}) collective-permute-start(f32[8,32,1,256]{3,1,0,2:T(8,128)S(1)} %get-tuple-element.50), channel_id=1, source_target_pairs={{0,4},{4,8},{8,12},{12,16},{16,20},{20,24},{24,28},{28,32},{32,36}... | collective-permute-start | bytes 786440 | tf_op jit(solution)/shard_map/ppermute | solution.py:24
  304.0 15.2 %collective-permute-start.7 = (f32[8,32,1,256]{3,1,0,2:T(8,128)S(1)}, f32[8,32,1,256]{3,1,0,2:T(8,128)S(1)}, u32[]{:S(2)}, u32[]{:S(2)}) collective-permute-start(f32[8,32,1,256]{3,1,0,2:T(8,128)S(1)} %get-tuple-element.51), channel_id=1, source_target_pairs={{4,0},{8,4},{12,8},{16,12},{20,16},{24,20},{28,24},{32,28},{36,32}... | collective-permute-start | bytes 786440 | tf_op jit(solution)/shard_map/ppermute | solution.py:25
  329.4 19.2 %collective-permute-start.9 = (f32[8,32,18,1]{1,0,3,2:T(8,128)}, f32[8,32,18,1]{1,0,3,2:T(8,128)}, u32[]{:S(2)}, u32[]{:S(2)}) collective-permute-start(f32[8,32,18,1]{1,0,3,2:T(8,128)} %copy.104), channel_id=1, source_target_pairs={{1,0},{2,1},{3,2},{5,4},{6,5},{7,6},{9,8},{10,9},{11,10},{13,12},{... | collective-permute-start | bytes 55304 | tf_op jit(solution)/shard_map/ppermute | solution.py:25
  330.8 14.6 %collective-permute-start.8 = (f32[8,32,18,1]{1,0,3,2:T(8,128)}, f32[8,32,18,1]{1,0,3,2:T(8,128)}, u32[]{:S(2)}, u32[]{:S(2)}) collective-permute-start(f32[8,32,18,1]{1,0,3,2:T(8,128)} %copy.101), channel_id=1, source_target_pairs={{0,1},{1,2},{2,3},{4,5},{5,6},{6,7},{8,9},{9,10},{10,11},{12,13},{... | collective-permute-start | bytes 55304 | tf_op jit(solution)/shard_map/ppermute | solution.py:24
  351.8 21.3 %copy-start.1 = (f32[4]{0:T(128)S(1)}, f32[4]{0:T(128)}, u32[]{:S(2)}) copy-start(f32[4]{0:T(128)} %param.19) | copy-start | bytes 52
  (11 other events, 59.6 us)
Sparse Core Ops, SparseCore 0:
  73.2 114.6 all-gather.2
where the time goes:
time: 381 us; the launch traced here: 380 us
  waiting for transfers between devices  199 us (52%)
  local copies, waits for them, and re-layouts  58.9 us (15%)
  starting transfers between devices  56.9 us (15%)
  other arithmetic  44.4 us (12%)
  between operations  14.5 us (4%)
  matrix products  5.87 us (2%)
    all_gather x1, waiting for transfers between devices, entering(): gathered = lax.all_gather(part, axis)  110 us
    all_to_all x1, waiting for transfers between devices, body(): lax.all_to_all(jnp.stack([wind_u, wind_v, lifted, eddy, mixing, density])...  63.8 us
    ppermute x5, waiting for transfers between devices, extended(): after = lax.ppermute(initial, axis, down)  25.6 us
    ppermute x5, starting transfers between devices, extended(): before = lax.ppermute(last, axis, up)  24 us
    all_to_all x1, starting transfers between devices, body(): lax.all_to_all(jnp.stack([wind_u, wind_v, lifted, eddy, mixing, density])...  19.2 us
    sub x1, other arithmetic, transport(): return conc - advect + spread + flux_above - flux  16.8 us
    ppermute x5, starting transfers between devices, extended(): after = lax.ppermute(initial, axis, down)  13.7 us
    slice x8, local copies, waits for them, and re-layouts, extended(): last = lax.slice_in_dim(array, length - width, length, axis=dim)  11.5 us
  transfers between devices with their start and end apart: 12, of which 6 were waited for; matrix products, arithmetic and copies ran while one was open for 9% of the time, Pallas kernels for 0%

commit v1 on v0

v1 whole, which is shorter than its diff:
```python
import functools

import jax
import jax.numpy as jnp
from jax import lax
from jax.experimental import pallas as pl
from jax.experimental.pallas import tpu as pltpu
from jax.sharding import PartitionSpec as P

MESH = pl.DeviceIdType.MESH
F32 = jnp.float32

diffuse_rate = 0.1
lift_scale = 0.1
lift_limit = 0.15
eddy_base = 0.005
eddy_slope = 0.03
mixing_base = 0.005
mixing_slope = 0.08
stable_weight = 20.0
level_decay = 32.0

G = 16
GRP = 4
GY = 4
LV = 2
NZ = 32
ROWS = 16
COLS = 256
MROWS = 256
BINS = 8
NSRC = 16


def kernel(
    u_ref, v_ref, t_ref, ash_ref, sx_ref, sy_ref, rate_ref, class_ref, table_ref,
    ash_out, met_out,
    uv, fields, conc, result, ret, coef, dens, marks,
    row_send, row_recv, col_send, col_recv, edge_send, edge_recv,
    arow_send, arow_recv, acol_send, acol_recv,
    bulk_s, bulk_r, edge_s, edge_r, ret_s, ret_r, near_s, near_r, local,
):
    grp, gx, gy = lax.axis_index("grp"), lax.axis_index("gx"), lax.axis_index("gy")
    line = grp * G + gx
    last_line = GRP * G - 1
    wrap_up, wrap_down = gx == G - 1, gx == 0
    row_up = (grp + wrap_up.astype(jnp.int32), lax.rem(gx + 1, G), gy)
    row_down = (grp - wrap_down.astype(jnp.int32), lax.rem(gx + G - 1, G), gy)

    met_in = [
        pltpu.make_async_copy(u_ref, uv.at[0], local.at[0]),
        pltpu.make_async_copy(v_ref, uv.at[1], local.at[1]),
    ]
    ash_in = pltpu.make_async_copy(ash_ref, conc, local.at[2])
    for copy in met_in:
        copy.start()
    ash_in.start()

    barrier = pltpu.get_barrier_semaphore()

    def greet(device):
        pl.semaphore_signal(barrier, inc=1, device_id=device, device_id_type=MESH)

    for d in range(1, G):
        greet((grp, jnp.bitwise_xor(gx, d), gy))
    pl.when(gy > 0)(lambda: greet((grp, gx, gy - 1)))
    pl.when(gy < GY - 1)(lambda: greet((grp, gx, gy + 1)))
    pl.when(grp > 0)(lambda: greet((grp - 1, gx, gy)))
    pl.when(grp < GRP - 1)(lambda: greet((grp + 1, gx, gy)))
    far_down = jnp.logical_and(wrap_down, grp > 0)
    far_up = jnp.logical_and(wrap_up, grp < GRP - 1)
    pl.when(far_down)(lambda: greet(row_down))
    pl.when(far_up)(lambda: greet(row_up))
    count = (
        G - 1
        + (gy > 0).astype(jnp.int32) + (gy < GY - 1).astype(jnp.int32)
        + (grp > 0).astype(jnp.int32) + (grp < GRP - 1).astype(jnp.int32)
        + far_down.astype(jnp.int32) + far_up.astype(jnp.int32)
    )
    pl.semaphore_wait(barrier, count)

    def remote(src, dst, send, recv, device):
        return pltpu.make_async_remote_copy(
            src_ref=src, dst_ref=dst, send_sem=send, recv_sem=recv,
            device_id=device, device_id_type=MESH,
        )

    sources = (u_ref, v_ref, t_ref)
    own_levels = pl.ds(LV * gx, LV)
    own_rows = pl.ds(pl.multiple_of(gx * ROWS, ROWS), ROWS)
    bulk = []
    for d in range(1, G):
        peer = jnp.bitwise_xor(gx, d)
        rows = pl.ds(pl.multiple_of(peer * ROWS, ROWS), ROWS)
        for f in range(3):
            copy = remote(
                sources[f].at[:, rows, :], fields.at[f, own_levels],
                bulk_s.at[f, d], bulk_r.at[f, d], (grp, peer, gy),
            )
            copy.start()
            bulk.append(copy)
    own_bulk = []
    for f in range(3):
        copy = pltpu.make_async_copy(
            sources[f].at[:, own_rows, :], fields.at[f, own_levels], local.at[3 + f]
        )
        copy.start()
        own_bulk.append(copy)

    lane = lax.broadcasted_iota(jnp.int32, (8, 128), 1)
    for copy in met_in:
        copy.wait()
    for f in range(2):
        for lev in range(LV):
            at = 2 * f + lev
            row_send[0, at : at + 1, :] = uv[f, lev, MROWS - 8 : MROWS, :][7:8]
            row_send[1, at : at + 1, :] = uv[f, lev, 0:8, :][0:1]
    row_send[0, 4:8, :] = jnp.zeros((4, COLS), F32)
    row_send[1, 4:8, :] = jnp.zeros((4, COLS), F32)

    def pack_columns(g, _):
        start = pl.multiple_of(g * ROWS, ROWS)
        right = jnp.zeros((8, 128), F32)
        left = jnp.zeros((8, 128), F32)
        for half in range(2):
            rows = pl.ds(start + 8 * half, 8)
            for f in range(2):
                for lev in range(LV):
                    c = 64 * half + 2 * f + lev
                    tail = uv[f, lev, rows, 128:256]
                    right = jnp.where(lane == c, pltpu.roll(tail, c + 1, 1), right)
                    head = uv[f, lev, rows, 0:128]
                    left = jnp.where(lane == c + 4, pltpu.roll(head, c + 4, 1), left)
        col_send[0, g] = right
        col_send[1, g] = left
        return 0

    lax.fori_loop(0, G, pack_columns, 0)

    rows_up = remote(row_send.at[0], row_recv.at[0], near_s.at[0], near_r.at[0], (grp + 1, gx, gy))
    rows_down = remote(row_send.at[1], row_recv.at[1], near_s.at[1], near_r.at[1], (grp - 1, gx, gy))
    cols_up = remote(col_send.at[0], col_recv.at[0], near_s.at[2], near_r.at[2], (grp, gx, gy + 1))
    cols_down = remote(col_send.at[1], col_recv.at[1], near_s.at[3], near_r.at[3], (grp, gx, gy - 1))

    def clear(ref):
        ref[...] = jnp.zeros(ref.shape, F32)

    pl.when(gy < GY - 1)(cols_up.start)
    pl.when(gy > 0)(cols_down.start)
    pl.when(grp < GRP - 1)(rows_up.start)
    pl.when(grp > 0)(rows_down.start)
    pl.when(grp == 0)(lambda: clear(row_recv.at[0]))
    pl.when(grp == GRP - 1)(lambda: clear(row_recv.at[1]))
    pl.when(gy == 0)(lambda: clear(col_recv.at[0]))
    pl.when(gy == GY - 1)(lambda: clear(col_recv.at[1]))

    def pack_rows(g, _):
        before = pl.ds(pl.multiple_of(jnp.maximum(g * ROWS - 8, 0), 8), 8)
        after = pl.ds(pl.multiple_of(jnp.minimum(g * ROWS + ROWS, MROWS - 8), 8), 8)
        for f in range(2):
            for lev in range(LV):
                at = 2 * f + lev
                edge_send[g, at : at + 1, 0:COLS] = uv[f, lev, before, :][7:8]
                edge_send[g, at + 4 : at + 5, 0:COLS] = uv[f, lev, after, :][0:1]
        return 0

    lax.fori_loop(0, G, pack_rows, 0)
    pl.when(grp > 0)(rows_up.wait_recv)
    pl.when(grp < GRP - 1)(rows_down.wait_recv)
    pl.when(gy > 0)(cols_up.wait_recv)
    pl.when(gy < GY - 1)(cols_down.wait_recv)
    edge_send[0, 0:4, 0:COLS] = row_recv[0, 0:4, :]
    edge_send[G - 1, 4:8, 0:COLS] = row_recv[1, 0:4, :]

    def merge_columns(g, _):
        edge_send[g, :, COLS : COLS + 128] = jnp.where(
            lane % 64 < 4, col_recv[0, g], col_recv[1, g]
        )
        return 0

    lax.fori_loop(0, G, merge_columns, 0)
    edges = []
    for d in range(1, G):
        peer = jnp.bitwise_xor(gx, d)
        copy = remote(
            edge_send.at[peer], edge_recv.at[gx], edge_s.at[d], edge_r.at[d], (grp, peer, gy)
        )
        copy.start()
        edges.append(copy)
    own_edge = pltpu.make_async_copy(edge_send.at[gx], edge_recv.at[gx], local.at[6])
    own_edge.start()

    row16 = lax.broadcasted_iota(jnp.int32, (ROWS, COLS), 0)
    lane16 = lax.broadcasted_iota(jnp.int32, (ROWS, COLS), 1)
    start_x, start_y = line * ROWS, gy * COLS

    def mark(s, _):
        hit = jnp.logical_and(row16 == sx_ref[s] - start_x, lane16 == sy_ref[s] - start_y)
        marks[s] = jnp.where(hit, 1.0, 0.0).astype(F32)
        return 0

    lax.fori_loop(0, NSRC, mark, 0)
    ash_in.wait()

    def emit(k, _):
        for b in range(BINS):
            total = conc[b, k]
            for s in range(NSRC):
                total = total + marks[s] * rate_ref[s, b, k]
            conc[b, k] = total
        return 0

    lax.fori_loop(0, NZ, emit, 0)

    lane128 = lax.broadcasted_iota(jnp.int32, (ROWS, 128), 1)

    def pack_ash(k, sums):
        sums = list(sums)
        for b in range(BINS):
            slab = conc[b, k]
            arow_send[0, b, pl.ds(k, 1), :] = slab[ROWS - 1 : ROWS]
            arow_send[1, b, pl.ds(k, 1), :] = slab[0:1]
            at = (b % 4) * NZ + k
            spot = lane128 == at
            right = pltpu.roll(slab[:, 128:256], lax.rem(at + 1, 128), 1)
            left = pltpu.roll(slab[:, 0:128], at, 1)
            sums[b // 4] = jnp.where(spot, right, sums[b // 4])
            sums[2 + b // 4] = jnp.where(spot, left, sums[2 + b // 4])
        return tuple(sums)

    packed = lax.fori_loop(0, NZ, pack_ash, tuple(jnp.zeros((ROWS, 128), F32) for _ in range(4)))
    for side in range(2):
        for part in range(2):
            acol_send[side, part] = packed[2 * side + part]

    arows_up = remote(arow_send.at[0], arow_recv.at[0], near_s.at[4], near_r.at[4], row_up)
    arows_down = remote(arow_send.at[1], arow_recv.at[1], near_s.at[5], near_r.at[5], row_down)
    acols_up = remote(acol_send.at[0], acol_recv.at[0], near_s.at[6], near_r.at[6], (grp, gx, gy + 1))
    acols_down = remote(acol_send.at[1], acol_recv.at[1], near_s.at[7], near_r.at[7], (grp, gx, gy - 1))
    pl.when(line < last_line)(arows_up.start)
    pl.when(line > 0)(arows_down.start)
    pl.when(gy < GY - 1)(acols_up.start)
    pl.when(gy > 0)(acols_down.start)
    pl.when(line == 0)(lambda: clear(arow_recv.at[0]))
    pl.when(line == last_line)(lambda: clear(arow_recv.at[1]))
    pl.when(gy == 0)(lambda: clear(acol_recv.at[0]))
    pl.when(gy == GY - 1)(lambda: clear(acol_recv.at[1]))

    for copy in bulk:
        copy.wait_recv()
    for copy in edges:
        copy.wait_recv()
    for copy in own_bulk:
        copy.wait()
    own_edge.wait()

    first_row, end_row = row16 == 0, row16 == ROWS - 1
    first_lane, end_lane = lane16 == 0, lane16 == COLS - 1

    def twice(half):
        return jnp.concatenate([half, half], axis=1)

    def along_x(field, below, above):
        east = jnp.where(end_row, above, pltpu.roll(field, ROWS - 1, 0))
        west = jnp.where(first_row, below, pltpu.roll(field, 1, 0))
        return east, west

    def along_y(field, below, above):
        north = jnp.where(end_lane, twice(above), pltpu.roll(field, COLS - 1, 1))
        south = jnp.where(first_lane, twice(below), pltpu.roll(field, 1, 1))
        return north, south

    def diagnose(g, total):
        edge_cols = edge_recv[g, :, COLS : COLS + 128]
        for lev in range(LV):
            k = LV * g + lev
            up, down = jnp.minimum(k + 1, NZ - 1), jnp.maximum(k - 1, 0)
            wind = []
            for f in range(2):
                at = 2 * f + lev
                field = fields[f, k]
                east, west = along_x(
                    field,
                    edge_recv[g, at : at + 1, 0:COLS],
                    edge_recv[g, at + 4 : at + 5, 0:COLS],
                )
                below = jnp.concatenate(
                    [pltpu.roll(edge_cols, (128 - at) % 128, 1), pltpu.roll(edge_cols, 64 - at, 1)], axis=0
                )
                above = jnp.concatenate(
                    [pltpu.roll(edge_cols, 127 - at - 4, 1), pltpu.roll(edge_cols, 63 - at - 4, 1)], axis=0
                )
                north, south = along_y(field, below, above)
                slope = 0.5 * (fields[f, up] - fields[f, down])
                wind.append((field, east, west, north, south, slope))
            warm = fields[2, k]
            warm_slope = 0.5 * (fields[2, up] - fields[2, down])
            (u, ue, uw, un, us, u_slope), (v, ve, vw, vn, vs, v_slope) = wind
            xstretch, yshear = 0.5 * (ue - uw), 0.5 * (un - us)
            xshear, ystretch = 0.5 * (ve - vw), 0.5 * (vn - vs)
            total = total + (xstretch + ystretch)
            lift = jnp.clip(-lift_scale * total, -lift_limit, lift_limit)
            ret[0, k] = u + diffuse_rate * (ue + uw + un + us - 4.0 * u) - lift * u_slope
            ret[1, k] = v + diffuse_rate * (ve + vw + vn + vs - 4.0 * v) - lift * v_slope
            ret[2, k] = warm - lift * warm_slope
            eddy = eddy_base + eddy_slope * jnp.sqrt((xstretch - ystretch) ** 2 + (yshear + xshear) ** 2)
            mixing = mixing_base + mixing_slope * jnp.sqrt(u_slope**2 + v_slope**2) / (
                1.0 + stable_weight * jnp.maximum(warm_slope, 0.0)
            )
            height = jnp.exp(jnp.zeros((1, COLS), F32) + k.astype(F32) * (1.0 / level_decay))
            dens[k] = jnp.sqrt(warm) * height
            coef[0, k] = eddy - jnp.minimum(u, 0.0)
            coef[1, k] = eddy + jnp.maximum(u, 0.0)
            coef[2, k] = eddy - jnp.minimum(v, 0.0)
            coef[3, k] = eddy + jnp.maximum(v, 0.0)
            coef[4, k] = mixing - jnp.minimum(lift, 0.0)
            coef[5, k] = mixing + jnp.maximum(lift, 0.0)
            coef[6, k] = 1.0 - (jnp.abs(u) + jnp.abs(v) + jnp.abs(lift) + 4.0 * eddy + 2.0 * mixing)
        return total

    lax.fori_loop(0, G, diagnose, jnp.zeros((ROWS, COLS), F32))
    dens[NZ] = jnp.zeros((ROWS, COLS), F32)

    returns = []
    for d in range(1, G):
        peer = jnp.bitwise_xor(gx, d)
        copy = remote(
            ret.at[:, pl.ds(LV * peer, LV)], met_out.at[:, :, own_rows, :],
            ret_s.at[d], ret_r.at[d], (grp, peer, gy),
        )
        copy.start()
        returns.append(copy)
    own_return = pltpu.make_async_copy(
        ret.at[:, own_levels], met_out.at[:, :, own_rows, :], local.at[7]
    )
    own_return.start()

    pl.when(line > 0)(arows_up.wait_recv)
    pl.when(line < last_line)(arows_down.wait_recv)
    pl.when(gy > 0)(acols_up.wait_recv)
    pl.when(gy < GY - 1)(acols_down.wait_recv)

    for b in range(BINS):
        speed = table_ref[class_ref[b]]

        def transport(k, _, b=b, speed=speed):
            here = conc[b, k]
            upper, lower = conc[b, jnp.minimum(k + 1, NZ - 1)], conc[b, jnp.maximum(k - 1, 0)]
            at = (b % 4) * NZ + k
            east, west = along_x(
                here, arow_recv[0, b, pl.ds(k, 1), :], arow_recv[1, b, pl.ds(k, 1), :]
            )
            below = pltpu.roll(acol_recv[0, b // 4], lax.rem(128 - at, 128), 1)
            above = pltpu.roll(acol_recv[1, b // 4], 127 - at, 1)
            north, south = along_y(here, below, above)
            out = here * (coef[6, k] - speed * dens[k]) + upper * (coef[4, k] + speed * dens[k + 1])
            out = out + east * coef[0, k] + west * coef[1, k]
            out = out + north * coef[2, k] + south * coef[3, k]
            result[b, k] = out + lower * coef[5, k]
            return 0

        lax.fori_loop(0, NZ, transport, 0)
        pltpu.make_async_copy(result.at[b], ash_out.at[b], local.at[8 + b]).start()

    for copy in returns:
        copy.wait_recv()
    own_return.wait()
    for b in range(BINS):
        pltpu.make_async_copy(result.at[b], ash_out.at[b], local.at[8 + b]).wait()
    for copy in bulk + edges + returns:
        copy.wait_send()
    pl.when(grp < GRP - 1)(rows_up.wait_send)
    pl.when(grp > 0)(rows_down.wait_send)
    pl.when(gy < GY - 1)(cols_up.wait_send)
    pl.when(gy > 0)(cols_down.wait_send)
    pl.when(line < last_line)(arows_up.wait_send)
    pl.when(line > 0)(arows_down.wait_send)
    pl.when(gy < GY - 1)(acols_up.wait_send)
    pl.when(gy > 0)(acols_down.wait_send)


def body(wind_u, wind_v, theta, ash, src_x, src_y, src_rate, settle_class, settle_table):
    hbm = pl.BlockSpec(memory_space=pl.ANY)
    smem = pl.BlockSpec(memory_space=pltpu.SMEM)
    dma = pltpu.SemaphoreType.DMA
    return tuple(
        pl.pallas_call(
            kernel,
            out_shape=(
                jax.ShapeDtypeStruct((BINS, NZ, ROWS, COLS), F32),
                jax.ShapeDtypeStruct((3, LV, MROWS, COLS), F32),
            ),
            in_specs=[hbm] * 4 + [smem] * 5,
            out_specs=(hbm, hbm),
            scratch_shapes=[
                pltpu.VMEM((2, LV, MROWS, COLS), F32),
                pltpu.VMEM((3, NZ, ROWS, COLS), F32),
                pltpu.VMEM((BINS, NZ, ROWS, COLS), F32),
                pltpu.VMEM((BINS, NZ, ROWS, COLS), F32),
                pltpu.VMEM((3, NZ, ROWS, COLS), F32),
                pltpu.VMEM((7, NZ, ROWS, COLS), F32),
                pltpu.VMEM((NZ + 1, ROWS, COLS), F32),
                pltpu.VMEM((NSRC, ROWS, COLS), F32),
                pltpu.VMEM((2, 8, COLS), F32),
                pltpu.VMEM((2, 8, COLS), F32),
                pltpu.VMEM((2, G, 8, 128), F32),
                pltpu.VMEM((2, G, 8, 128), F32),
                pltpu.VMEM((G, 8, COLS + 128), F32),
                pltpu.VMEM((G, 8, COLS + 128), F32),
                pltpu.VMEM((2, BINS, NZ, COLS), F32),
                pltpu.VMEM((2, BINS, NZ, COLS), F32),
                pltpu.VMEM((2, 2, ROWS, 128), F32),
                pltpu.VMEM((2, 2, ROWS, 128), F32),
                dma((3, G)), dma((3, G)),
                dma((G,)), dma((G,)),
                dma((G,)), dma((G,)),
                dma((8,)), dma((8,)),
                dma((16,)),
            ],
            compiler_params=pltpu.CompilerParams(
                collective_id=0, has_side_effects=True, vmem_limit_bytes=40 * 2**20
            ),
        )(wind_u, wind_v, theta, ash, src_x, src_y, src_rate, settle_class, settle_table)
    )


def solution(mesh):
    in_specs = (
        P("gx", "grp", "gy"),
        P("gx", "grp", "gy"),
        P("gx", "grp", "gy"),
        P(None, None, ("grp", "gx"), "gy"),
        P(),
        P(),
        P(),
        P(),
        P(),
    )
    out_specs = (P(None, None, ("grp", "gx"), "gy"), P(None, "gx", "grp", "gy"))
    return jax.shard_map(body, mesh=mesh, in_specs=in_specs, out_specs=out_specs, check_vma=False)
```

time: 381 us -> 108 us (0.28)
  waiting for transfers between devices: 199 us -> 0 us
  Pallas kernels: 0 us -> 94.2 us
  starting transfers between devices: 56.9 us -> 0 us
  local copies, waits for them, and re-layouts: 58.9 us -> 11.9 us
  other arithmetic: 44.4 us -> 0 us
  between operations: 14.5 us -> 0.66 us
  matrix products: 5.87 us -> 0 us
    all_gather x1 -> x0, waiting for transfers between devices: 110 us -> none  [entering(): gathered = lax.all_gather(part, axis)]
    pallas_call x0 -> x1, Pallas kernels: none -> 94.2 us  [body(): pl.pallas_call(kernel, out_shape=(jax.ShapeDtypeStruct((BINS, NZ, ROWS, C...]
    all_to_all x1 -> x0, waiting for transfers between devices: 63.8 us -> none  [body(): lax.all_to_all(jnp.stack([wind_u, wind_v, lifted, eddy, mixing, density])...]
    ppermute x10 -> x0, starting transfers between devices: 37.7 us -> none  [the longest x5 24 us: extended(): before = lax.ppermute(last, axis, up)]
    slice x14 -> x0, local copies, waits for them, and re-layouts: 27 us -> none  [the longest x8 11.5 us: extended(): last = lax.slice_in_dim(array, length - width, length, axis=dim)]
    ppermute x10 -> x0, waiting for transfers between devices: 25.6 us -> none  [the longest x5 25.6 us: extended(): after = lax.ppermute(initial, axis, down)]
    sub x4 -> x0, other arithmetic: 22.6 us -> none  [the longest x1 16.8 us: transport(): return conc - advect + spread + flux_above - flux]
    all_to_all x1 -> x0, starting transfers between devices: 19.2 us -> none  [body(): lax.all_to_all(jnp.stack([wind_u, wind_v, lifted, eddy, mixing, density])...]
  transfers between devices with their start and end apart: 12 -> 0, of which waited for: 6 -> 0; matrix products, arithmetic and copies ran while one was open for 9% -> 0% of each run, Pallas kernels for 0% -> 0%
where the time goes in v1:
time: 108 us; the launch traced here: 107 us
  Pallas kernels  94.2 us (87%)
  local copies, waits for them, and re-layouts  11.9 us (11%)
    pallas_call x1, Pallas kernels, body(): pl.pallas_call(kernel, out_shape=(jax.ShapeDtypeStruct((BINS, NZ, ROWS, C...  94.2 us
    unnamed x20, local copies, waits for them, and re-layouts  11.9 us

profile of v1, /device:TPU:1, one launch (start us, length us, event | category | flops | bytes accessed | tf_op | source)
XLA Modules:
  0.0 106.8 jit_solution(9032609015724871469)
XLA Ops:
  0.6 0.0 copy-start
  0.6 2.2 %copy-done = f32[8,32,16,256]{3,2,1,0:T(8,128)S(1)} copy-done((f32[8,32,16,256]{3,2,1,0:T(8,128)S(1)}, f32[8,32,16,256]{3,2,1,0:T(8,128)}, u32[]{:S(2)}) %copy-start) | copy-done | bytes 4194328
  2.8 0.0 copy-start.1
  2.8 1.0 copy-done.1
  3.9 0.0 copy-start.2
  3.9 1.0 copy-done.2
  4.9 0.0 copy-start.3
  4.9 1.0 copy-done.3
  5.9 0.0 copy-start.4
  6.0 0.8 copy-done.4
  6.8 0.0 copy-start.5
  6.8 0.7 copy-done.5
  7.4 0.0 copy-start.6
  7.4 0.7 copy-done.6
  8.1 0.0 copy-start.7
  8.1 0.7 copy-done.7
  8.8 0.0 copy-start.8
  8.8 0.7 copy-done.8
  9.4 94.2 %shard_map.104 = (f32[8,32,16,256]{3,2,1,0:T(8,128)S(1)}, f32[3,2,256,256]{3,2,1,0:T(8,128)S(1)}) custom-call(f32[2,256,256]{2,1,0:T(8,128)S(1)} %copy-done.1, f32[2,256,256]{2,1,0:T(8,128)S(1)} %copy-done.2, f32[2,256,256]{2,1,0:T(8,128)S(1)} %copy-done.3, f32[8,32,16,256]{3,2,1,0:T(8,128)S(1)} %copy-done, s32[16]{0:T(128)S(1)} %copy-done.5, ...), custom_call_target="tpu_custom_call" | custom-call | tf_op jit(solution)/shard_map/pallas_call | solution.py:387
  103.6 2.0 %copy.13 = f32[8,32,16,256]{3,2,1,0:T(8,128)} copy(f32[8,32,16,256]{3,2,1,0:T(8,128)S(1)} %get-tuple-element.4) | data formatting | bytes 8388608
  105.6 1.1 %copy.14 = f32[3,2,256,256]{3,2,1,0:T(8,128)} copy(f32[3,2,256,256]{3,2,1,0:T(8,128)S(1)} %get-tuple-element.5) | data formatting | bytes 3145728
Async XLA Ops:
  0.6 2.2 %copy-start = (f32[8,32,16,256]{3,2,1,0:T(8,128)S(1)}, f32[8,32,16,256]{3,2,1,0:T(8,128)}, u32[]{:S(2)}) copy-start(f32[8,32,16,256]{3,2,1,0:T(8,128)} %ash_ref.1) | copy-start | bytes 12582916
  2.8 1.0 copy-start.1
  3.9 1.0 copy-start.2
  4.9 1.0 copy-start.3
  5.9 0.8 copy-start.4
  6.8 0.7 copy-start.5
  7.4 0.7 copy-start.6
  8.1 0.7 copy-start.7
  8.8 0.7 copy-start.8

commit v2 on v1

--- a/solution.py
+++ b/solution.py
@@ -33,12 +33,13 @@
 
 
 def kernel(
-    u_ref, v_ref, t_ref, ash_ref, sx_ref, sy_ref, rate_ref, class_ref, table_ref,
+    u_ref, v_ref, t_ref, ash_ref, sx_hbm, sy_hbm, rate_hbm, class_hbm, table_hbm,
     ash_out, met_out,
-    uv, fields, conc, result, ret, coef, dens, marks,
+    sx_ref, sy_ref, rate_ref, class_ref, table_ref,
+    met, partner, lift_recv, fields, conc, ret, lifts, coef, dens, marks,
     row_send, row_recv, col_send, col_recv, edge_send, edge_recv,
     arow_send, arow_recv, acol_send, acol_recv,
-    bulk_s, bulk_r, edge_s, edge_r, ret_s, ret_r, near_s, near_r, local,
+    bulk_s, bulk_r, edge_s, edge_r, ret_s, ret_r, lift_s, lift_r, part_s, part_r, near_s, near_r, local,
 ):
     grp, gx, gy = lax.axis_index("grp"), lax.axis_index("gx"), lax.axis_index("gy")
     line = grp * G + gx
@@ -47,14 +48,20 @@
     row_up = (grp + wrap_up.astype(jnp.int32), lax.rem(gx + 1, G), gy)
     row_down = (grp - wrap_down.astype(jnp.int32), lax.rem(gx + G - 1, G), gy)
 
-    met_in = [
-        pltpu.make_async_copy(u_ref, uv.at[0], local.at[0]),
-        pltpu.make_async_copy(v_ref, uv.at[1], local.at[1]),
+    sources = (u_ref, v_ref, t_ref)
+    met_in = [pltpu.make_async_copy(sources[f], met.at[f], local.at[f]) for f in range(3)]
+    ash_in = pltpu.make_async_copy(ash_ref, conc, local.at[3])
+    small_in = [
+        pltpu.make_async_copy(src, dst, local.at[8 + i])
+        for i, (src, dst) in enumerate(
+            (
+                (sx_hbm, sx_ref), (sy_hbm, sy_ref), (rate_hbm, rate_ref),
+                (class_hbm, class_ref), (table_hbm, table_ref),
+            )
+        )
     ]
-    ash_in = pltpu.make_async_copy(ash_ref, conc, local.at[2])
-    for copy in met_in:
+    for copy in met_in + [ash_in] + small_in:
         copy.start()
-    ash_in.start()
 
     barrier = pltpu.get_barrier_semaphore()
 
@@ -85,16 +92,14 @@
             device_id=device, device_id_type=MESH,
         )
 
-    sources = (u_ref, v_ref, t_ref)
     own_levels = pl.ds(LV * gx, LV)
-    own_rows = pl.ds(pl.multiple_of(gx * ROWS, ROWS), ROWS)
+    own_x, own_z = gx // 4, gx % 4
     bulk = []
     for d in range(1, G):
         peer = jnp.bitwise_xor(gx, d)
-        rows = pl.ds(pl.multiple_of(peer * ROWS, ROWS), ROWS)
         for f in range(3):
             copy = remote(
-                sources[f].at[:, rows, :], fields.at[f, own_levels],
+                sources[f].at[:, peer // 4, peer % 4], fields.at[f, own_levels],
                 bulk_s.at[f, d], bulk_r.at[f, d], (grp, peer, gy),
             )
             copy.start()
@@ -102,10 +107,23 @@
     own_bulk = []
     for f in range(3):
         copy = pltpu.make_async_copy(
-            sources[f].at[:, own_rows, :], fields.at[f, own_levels], local.at[3 + f]
+            sources[f].at[:, own_x, own_z], fields.at[f, own_levels], local.at[4 + f]
         )
         copy.start()
         own_bulk.append(copy)
+
+    mine = 1 - gx % 2
+    mate = jnp.bitwise_xor(gx, 1)
+    pairs = []
+    for j in range(1, 4):
+        group = jnp.bitwise_xor(mate % 4, j)
+        for f in range(3):
+            copy = remote(
+                sources[f].at[mine, :, group], partner.at[f, :, group],
+                part_s.at[f, j], part_r.at[f, j], (grp, mate, gy),
+            )
+            copy.start()
+            pairs.append(copy)
 
     lane = lax.broadcasted_iota(jnp.int32, (8, 128), 1)
     for copy in met_in:
@@ -113,23 +131,22 @@
     for f in range(2):
         for lev in range(LV):
             at = 2 * f + lev
-            row_send[0, at : at + 1, :] = uv[f, lev, MROWS - 8 : MROWS, :][7:8]
-            row_send[1, at : at + 1, :] = uv[f, lev, 0:8, :][0:1]
+            row_send[0, at : at + 1, :] = met[f, lev, 3, 3, ROWS - 1 : ROWS, :]
+            row_send[1, at : at + 1, :] = met[f, lev, 0, 0, 0:1, :]
     row_send[0, 4:8, :] = jnp.zeros((4, COLS), F32)
     row_send[1, 4:8, :] = jnp.zeros((4, COLS), F32)
 
     def pack_columns(g, _):
-        start = pl.multiple_of(g * ROWS, ROWS)
         right = jnp.zeros((8, 128), F32)
         left = jnp.zeros((8, 128), F32)
         for half in range(2):
-            rows = pl.ds(start + 8 * half, 8)
+            rows = slice(8 * half, 8 * half + 8)
             for f in range(2):
                 for lev in range(LV):
                     c = 64 * half + 2 * f + lev
-                    tail = uv[f, lev, rows, 128:256]
+                    tail = met[f, lev, g // 4, g % 4, rows, 128:256]
                     right = jnp.where(lane == c, pltpu.roll(tail, c + 1, 1), right)
-                    head = uv[f, lev, rows, 0:128]
+                    head = met[f, lev, g // 4, g % 4, rows, 0:128]
                     left = jnp.where(lane == c + 4, pltpu.roll(head, c + 4, 1), left)
         col_send[0, g] = right
         col_send[1, g] = left
@@ -155,13 +172,12 @@
     pl.when(gy == GY - 1)(lambda: clear(col_recv.at[1]))
 
     def pack_rows(g, _):
-        before = pl.ds(pl.multiple_of(jnp.maximum(g * ROWS - 8, 0), 8), 8)
-        after = pl.ds(pl.multiple_of(jnp.minimum(g * ROWS + ROWS, MROWS - 8), 8), 8)
+        before, after = jnp.maximum(g - 1, 0), jnp.minimum(g + 1, G - 1)
         for f in range(2):
             for lev in range(LV):
                 at = 2 * f + lev
-                edge_send[g, at : at + 1, 0:COLS] = uv[f, lev, before, :][7:8]
-                edge_send[g, at + 4 : at + 5, 0:COLS] = uv[f, lev, after, :][0:1]
+                edge_send[g, at : at + 1, 0:COLS] = met[f, lev, before // 4, before % 4, ROWS - 1 : ROWS, :]
+                edge_send[g, at + 4 : at + 5, 0:COLS] = met[f, lev, after // 4, after % 4, 0:1, :]
         return 0
 
     lax.fori_loop(0, G, pack_rows, 0)
@@ -187,12 +203,15 @@
         )
         copy.start()
         edges.append(copy)
-    own_edge = pltpu.make_async_copy(edge_send.at[gx], edge_recv.at[gx], local.at[6])
+    own_edge = pltpu.make_async_copy(edge_send.at[gx], edge_recv.at[gx], local.at[7])
     own_edge.start()
 
     row16 = lax.broadcasted_iota(jnp.int32, (ROWS, COLS), 0)
     lane16 = lax.broadcasted_iota(jnp.int32, (ROWS, COLS), 1)
     start_x, start_y = line * ROWS, gy * COLS
+
+    for copy in small_in:
+        copy.wait()
 
     def mark(s, _):
         hit = jnp.logical_and(row16 == sx_ref[s] - start_x, lane16 == sy_ref[s] - start_y)
@@ -303,6 +322,7 @@
             ret[0, k] = u + diffuse_rate * (ue + uw + un + us - 4.0 * u) - lift * u_slope
             ret[1, k] = v + diffuse_rate * (ve + vw + vn + vs - 4.0 * v) - lift * v_slope
             ret[2, k] = warm - lift * warm_slope
+            lifts[k] = lift
             eddy = eddy_base + eddy_slope * jnp.sqrt((xstretch - ystretch) ** 2 + (yshear + xshear) ** 2)
             mixing = mixing_base + mixing_slope * jnp.sqrt(u_slope**2 + v_slope**2) / (
                 1.0 + stable_weight * jnp.maximum(warm_slope, 0.0)
@@ -321,31 +341,46 @@
     lax.fori_loop(0, G, diagnose, jnp.zeros((ROWS, COLS), F32))
     dens[NZ] = jnp.zeros((ROWS, COLS), F32)
 
-    returns = []
+    lift_back, back = [], []
     for d in range(1, G):
         peer = jnp.bitwise_xor(gx, d)
-        copy = remote(
-            ret.at[:, pl.ds(LV * peer, LV)], met_out.at[:, :, own_rows, :],
-            ret_s.at[d], ret_r.at[d], (grp, peer, gy),
-        )
+        if d % 4:
+            copy = remote(
+                lifts.at[LV * peer + 1 - peer % 2], lift_recv.at[own_x, own_z],
+                lift_s.at[d], lift_r.at[d], (grp, peer, gy),
+            )
+            copy.start()
+            lift_back.append(copy)
+    for d in range(1, G):
+        peer = jnp.bitwise_xor(gx, d)
+        if d % 4:
+            copy = remote(
+                ret.at[:, LV * peer + peer % 2], met_out.at[:, peer % 2, own_x, own_z],
+                ret_s.at[d], ret_r.at[d], (grp, peer, gy),
+            )
+        else:
+            copy = remote(
+                ret.at[:, pl.ds(LV * peer, LV)], met_out.at[:, :, own_x, own_z],
+                ret_s.at[d], ret_r.at[d], (grp, peer, gy),
+            )
         copy.start()
-        returns.append(copy)
-    own_return = pltpu.make_async_copy(
-        ret.at[:, own_levels], met_out.at[:, :, own_rows, :], local.at[7]
+        back.append(copy)
+    own_back = pltpu.make_async_copy(
+        ret.at[:, own_levels], met_out.at[:, :, own_x, own_z], local.at[13]
     )
-    own_return.start()
+    own_back.start()
 
     pl.when(line > 0)(arows_up.wait_recv)
     pl.when(line < last_line)(arows_down.wait_recv)
     pl.when(gy > 0)(acols_up.wait_recv)
     pl.when(gy < GY - 1)(acols_down.wait_recv)
 
-    for b in range(BINS):
-        speed = table_ref[class_ref[b]]
-
-        def transport(k, _, b=b, speed=speed):
+    speeds = [table_ref[class_ref[b]] for b in range(BINS)]
+
+    def transport(k, _):
+        up, down = jnp.minimum(k + 1, NZ - 1), jnp.maximum(k - 1, 0)
+        for b in range(BINS):
             here = conc[b, k]
-            upper, lower = conc[b, jnp.minimum(k + 1, NZ - 1)], conc[b, jnp.maximum(k - 1, 0)]
             at = (b % 4) * NZ + k
             east, west = along_x(
                 here, arow_recv[0, b, pl.ds(k, 1), :], arow_recv[1, b, pl.ds(k, 1), :]
@@ -353,21 +388,53 @@
             below = pltpu.roll(acol_recv[0, b // 4], lax.rem(128 - at, 128), 1)
             above = pltpu.roll(acol_recv[1, b // 4], 127 - at, 1)
             north, south = along_y(here, below, above)
-            out = here * (coef[6, k] - speed * dens[k]) + upper * (coef[4, k] + speed * dens[k + 1])
+            out = here * (coef[6, k] - speeds[b] * dens[k])
+            out = out + conc[b, up] * (coef[4, k] + speeds[b] * dens[k + 1])
             out = out + east * coef[0, k] + west * coef[1, k]
             out = out + north * coef[2, k] + south * coef[3, k]
-            result[b, k] = out + lower * coef[5, k]
-            return 0
-
-        lax.fori_loop(0, NZ, transport, 0)
-        pltpu.make_async_copy(result.at[b], ash_out.at[b], local.at[8 + b]).start()
-
-    for copy in returns:
+            ash_out[b, k] = out + conc[b, down] * coef[5, k]
+        return 0
+
+    lax.fori_loop(0, NZ, transport, 0)
+
+    for copy in pairs + lift_back:
         copy.wait_recv()
-    own_return.wait()
-    for b in range(BINS):
-        pltpu.make_async_copy(result.at[b], ash_out.at[b], local.at[8 + b]).wait()
-    for copy in bulk + edges + returns:
+    half = jnp.where(gx % 2 == 0, 0.5, -0.5).astype(F32)
+
+    def step_rows(x, _):
+        for j in range(1, 4):
+            z = jnp.bitwise_xor(own_z, j)
+            g = 4 * x + z
+            edge_cols = edge_send[g, :, COLS : COLS + 128]
+            lift = lift_recv[x, z]
+            for f in range(3):
+                field = met[f, mine, x, z]
+                slope = half * (partner[f, x, z] - met[f, 1 - mine, x, z])
+                after = field - lift * slope
+                if f < 2:
+                    at = 2 * f + mine
+                    east, west = along_x(
+                        field,
+                        edge_send[g, pl.ds(at, 1), 0:COLS],
+                        edge_send[g, pl.ds(at + 4, 1), 0:COLS],
+                    )
+                    below = jnp.concatenate(
+                        [pltpu.roll(edge_cols, 128 - at, 1), pltpu.roll(edge_cols, 64 - at, 1)], axis=0
+                    )
+                    above = jnp.concatenate(
+                        [pltpu.roll(edge_cols, 123 - at, 1), pltpu.roll(edge_cols, 59 - at, 1)], axis=0
+                    )
+                    north, south = along_y(field, below, above)
+                    after = after + diffuse_rate * (east + west + north + south - 4.0 * field)
+                met_out[f, mine, x, z] = after
+        return 0
+
+    lax.fori_loop(0, 4, step_rows, 0)
+
+    for copy in back:
+        copy.wait_recv()
+    own_back.wait()
+    for copy in bulk + pairs + edges + lift_back + back:
         copy.wait_send()
     pl.when(grp < GRP - 1)(rows_up.wait_send)
     pl.when(grp > 0)(rows_down.wait_send)
@@ -380,24 +447,31 @@
 
 
 def body(wind_u, wind_v, theta, ash, src_x, src_y, src_rate, settle_class, settle_table):
-    hbm = pl.BlockSpec(memory_space=pl.ANY)
-    smem = pl.BlockSpec(memory_space=pltpu.SMEM)
+    hbm = pl.BlockSpec(memory_space=pltpu.HBM)
+    vmem = pl.BlockSpec(memory_space=pltpu.VMEM)
     dma = pltpu.SemaphoreType.DMA
-    return tuple(
-        pl.pallas_call(
+    tiled = (LV, 4, 4, ROWS, COLS)
+    ash_next, met_next = pl.pallas_call(
             kernel,
             out_shape=(
-                jax.ShapeDtypeStruct((BINS, NZ, ROWS, COLS), F32),
-                jax.ShapeDtypeStruct((3, LV, MROWS, COLS), F32),
+                pltpu.VMEM((BINS, NZ, ROWS, COLS), F32),
+                pltpu.VMEM((3,) + tiled, F32),
             ),
-            in_specs=[hbm] * 4 + [smem] * 5,
-            out_specs=(hbm, hbm),
+            in_specs=[hbm] * 9,
+            out_specs=(vmem, vmem),
             scratch_shapes=[
-                pltpu.VMEM((2, LV, MROWS, COLS), F32),
+                pltpu.SMEM((NSRC,), jnp.int32),
+                pltpu.SMEM((NSRC,), jnp.int32),
+                pltpu.SMEM((NSRC, BINS, NZ), F32),
+                pltpu.SMEM(settle_class.shape, jnp.int32),
+                pltpu.SMEM(settle_table.shape, F32),
+                pltpu.VMEM((3,) + tiled, F32),
+                pltpu.VMEM((3,) + tiled[1:], F32),
+                pltpu.VMEM(tiled[1:], F32),
                 pltpu.VMEM((3, NZ, ROWS, COLS), F32),
                 pltpu.VMEM((BINS, NZ, ROWS, COLS), F32),
-                pltpu.VMEM((BINS, NZ, ROWS, COLS), F32),
                 pltpu.VMEM((3, NZ, ROWS, COLS), F32),
+                pltpu.VMEM((NZ, ROWS, COLS), F32),
                 pltpu.VMEM((7, NZ, ROWS, COLS), F32),
                 pltpu.VMEM((NZ + 1, ROWS, COLS), F32),
                 pltpu.VMEM((NSRC, ROWS, COLS), F32),
@@ -414,14 +488,24 @@
                 dma((3, G)), dma((3, G)),
                 dma((G,)), dma((G,)),
                 dma((G,)), dma((G,)),
+                dma((G,)), dma((G,)),
+                dma((3, 4)), dma((3, 4)),
                 dma((8,)), dma((8,)),
-                dma((16,)),
+                dma((14,)),
             ],
             compiler_params=pltpu.CompilerParams(
-                collective_id=0, has_side_effects=True, vmem_limit_bytes=40 * 2**20
+                collective_id=0, has_side_effects=True, vmem_limit_bytes=48 * 2**20
             ),
-        )(wind_u, wind_v, theta, ash, src_x, src_y, src_rate, settle_class, settle_table)
+    )(
+        *(
+            pltpu.with_memory_space_constraint(array, pltpu.HBM)
+            for array in (
+                wind_u.reshape(tiled), wind_v.reshape(tiled), theta.reshape(tiled), ash,
+                src_x, src_y, src_rate, settle_class, settle_table,
+            )
+        )
     )
+    return ash_next, met_next.reshape(3, LV, MROWS, COLS)
 
 
 def solution(mesh):

time: 108 us -> 91.6 us (0.85); the launches traced: 107 us -> 91.6 us
  local copies, waits for them, and re-layouts: 11.9 us -> 3.16 us
  Pallas kernels: 94.2 us -> 87.8 us
    unnamed x20 -> x2, local copies, waits for them, and re-layouts: 11.9 us -> 3.16 us
    pallas_call x1, Pallas kernels: 94.2 us -> 87.8 us  [body(): pl.pallas_call(kernel, out_shape=(pltpu.VMEM((BINS, NZ, ROWS, COLS), F32)...]
where the time goes in v2:
time: 91.6 us
  Pallas kernels  87.8 us (96%)
  local copies, waits for them, and re-layouts  3.16 us (3%)
    pallas_call x1, Pallas kernels, body(): pl.pallas_call(kernel, out_shape=(pltpu.VMEM((BINS, NZ, ROWS, COLS), F32)...  87.8 us
    unnamed x2, local copies, waits for them, and re-layouts  3.16 us

profile of v2, /device:TPU:1, one launch (start us, length us, event | category | flops | bytes accessed | tf_op | source)
XLA Modules:
  0.0 91.6 jit_solution(10338870884648422412)
XLA Ops:
  0.6 87.8 %shard_map.104 = (f32[8,32,16,256]{3,2,1,0:T(8,128)S(1)}, f32[3,2,4,4,16,256]{5,4,3,2,1,0:T(8,128)S(1)}) custom-call(f32[2,4,4,16,256]{4,3,2,1,0:T(8,128)} %bitcast.5, f32[2,4,4,16,256]{4,3,2,1,0:T(8,128)} %bitcast.6, f32[2,4,4,16,256]{4,3,2,1,0:T(8,128)} %bitcast.7, f32[8,32,16,256]{3,2,1,0:T(8,128)} %ash_ref.1, s32[16]{0:T(128)} %sx_hbm.1, s32[16]{0:T(128)} %sy_hbm.1, ...), custom_call_target="tpu_custom_call" | custom-call | tf_op jit(solution)/shard_map/pallas_call | solution.py:454
  88.4 2.0 %copy.13 = f32[8,32,16,256]{3,2,1,0:T(8,128)} copy(f32[8,32,16,256]{3,2,1,0:T(8,128)S(1)} %get-tuple-element.6) | data formatting | bytes 8388608
  90.4 1.1 %copy.14 = f32[3,2,256,256]{3,2,1,0:T(8,128)} copy(f32[3,2,256,256]{3,2,1,0:T(8,128)S(1)} %bitcast.4) | data formatting | bytes 3145728

commit v3 on v2

--- a/solution.py
+++ b/solution.py
@@ -36,10 +36,10 @@
     u_ref, v_ref, t_ref, ash_ref, sx_hbm, sy_hbm, rate_hbm, class_hbm, table_hbm,
     ash_out, met_out,
     sx_ref, sy_ref, rate_ref, class_ref, table_ref,
-    met, partner, lift_recv, fields, conc, ret, lifts, coef, dens, marks,
+    met, partner, cum_recv, fields, conc, ret, cums, coef, dens, marks,
     row_send, row_recv, col_send, col_recv, edge_send, edge_recv,
     arow_send, arow_recv, acol_send, acol_recv,
-    bulk_s, bulk_r, edge_s, edge_r, ret_s, ret_r, lift_s, lift_r, part_s, part_r, near_s, near_r, local,
+    bulk_s, bulk_r, edge_s, edge_r, ret_s, ret_r, cum_s, cum_r, mate_s, mate_r, part_s, part_r, near_s, near_r, local,
 ):
     grp, gx, gy = lax.axis_index("grp"), lax.axis_index("gx"), lax.axis_index("gy")
     line = grp * G + gx
@@ -68,7 +68,7 @@
     def greet(device):
         pl.semaphore_signal(barrier, inc=1, device_id=device, device_id_type=MESH)
 
-    for d in range(1, G):
+    for d in range(G - 1, 0, -1):
         greet((grp, jnp.bitwise_xor(gx, d), gy))
     pl.when(gy > 0)(lambda: greet((grp, gx, gy - 1)))
     pl.when(gy < GY - 1)(lambda: greet((grp, gx, gy + 1)))
@@ -115,14 +115,13 @@
     mine = 1 - gx % 2
     mate = jnp.bitwise_xor(gx, 1)
     pairs = []
-    for j in range(1, 4):
+    for j in range(2, 4):
         group = jnp.bitwise_xor(mate % 4, j)
         for f in range(3):
             copy = remote(
                 sources[f].at[mine, :, group], partner.at[f, :, group],
                 part_s.at[f, j], part_r.at[f, j], (grp, mate, gy),
             )
-            copy.start()
             pairs.append(copy)
 
     lane = lax.broadcasted_iota(jnp.int32, (8, 128), 1)
@@ -265,6 +264,10 @@
     pl.when(gy == 0)(lambda: clear(acol_recv.at[0]))
     pl.when(gy == GY - 1)(lambda: clear(acol_recv.at[1]))
 
+    for copy in bulk:
+        copy.wait_send()
+    for copy in pairs:
+        copy.start()
     for copy in bulk:
         copy.wait_recv()
     for copy in edges:
@@ -322,7 +325,8 @@
             ret[0, k] = u + diffuse_rate * (ue + uw + un + us - 4.0 * u) - lift * u_slope
             ret[1, k] = v + diffuse_rate * (ve + vw + vn + vs - 4.0 * v) - lift * v_slope
             ret[2, k] = warm - lift * warm_slope
-            lifts[k] = lift
+            if lev == 1:
+                cums[g] = total
             eddy = eddy_base + eddy_slope * jnp.sqrt((xstretch - ystretch) ** 2 + (yshear + xshear) ** 2)
             mixing = mixing_base + mixing_slope * jnp.sqrt(u_slope**2 + v_slope**2) / (
                 1.0 + stable_weight * jnp.maximum(warm_slope, 0.0)
@@ -341,19 +345,22 @@
     lax.fori_loop(0, G, diagnose, jnp.zeros((ROWS, COLS), F32))
     dens[NZ] = jnp.zeros((ROWS, COLS), F32)
 
-    lift_back, back = [], []
+    near = jnp.logical_or(own_z == 1, own_z == 2)
+    near_z = jnp.where(own_z < 2, 2, 1)
+    half_z = jnp.where(own_z < 2, 2, 0)
+    cum_back = []
+    for dx in range(4):
+        peer = 4 * jnp.bitwise_xor(own_x, dx) + near_z
+        copy = remote(
+            cums.at[2 * (peer // 2)], cum_recv.at[own_x, own_z],
+            cum_s.at[dx], cum_r.at[own_z % 2, dx], (grp, peer, gy),
+        )
+        copy.start()
+        cum_back.append(copy)
+    back = []
     for d in range(1, G):
         peer = jnp.bitwise_xor(gx, d)
-        if d % 4:
-            copy = remote(
-                lifts.at[LV * peer + 1 - peer % 2], lift_recv.at[own_x, own_z],
-                lift_s.at[d], lift_r.at[d], (grp, peer, gy),
-            )
-            copy.start()
-            lift_back.append(copy)
-    for d in range(1, G):
-        peer = jnp.bitwise_xor(gx, d)
-        if d % 4:
+        if d % 4 > 1:
             copy = remote(
                 ret.at[:, LV * peer + peer % 2], met_out.at[:, peer % 2, own_x, own_z],
                 ret_s.at[d], ret_r.at[d], (grp, peer, gy),
@@ -397,35 +404,57 @@
 
     lax.fori_loop(0, NZ, transport, 0)
 
-    for copy in pairs + lift_back:
+    hand_on = remote(
+        cum_recv.at[:, pl.ds(half_z, 2)], cum_recv.at[:, pl.ds(half_z, 2)],
+        mate_s.at[0], mate_r.at[0], (grp, mate, gy),
+    )
+
+    @pl.when(near)
+    def _():
+        for parity in range(2):
+            for dx in range(4):
+                remote(
+                    cums.at[0], cum_recv.at[own_x, own_z], cum_s.at[dx], cum_r.at[parity, dx], (grp, mate, gy)
+                ).wait_recv()
+        hand_on.start()
+
+    pl.when(jnp.logical_not(near))(hand_on.wait_recv)
+    for copy in pairs:
         copy.wait_recv()
     half = jnp.where(gx % 2 == 0, 0.5, -0.5).astype(F32)
+    above_cum = (gx % 2).astype(F32)
 
     def step_rows(x, _):
-        for j in range(1, 4):
+        for j in range(2, 4):
             z = jnp.bitwise_xor(own_z, j)
             g = 4 * x + z
             edge_cols = edge_send[g, :, COLS : COLS + 128]
-            lift = lift_recv[x, z]
+            wind = []
+            for f in range(2):
+                field = met[f, mine, x, z]
+                at = 2 * f + mine
+                east, west = along_x(
+                    field,
+                    edge_send[g, pl.ds(at, 1), 0:COLS],
+                    edge_send[g, pl.ds(at + 4, 1), 0:COLS],
+                )
+                below = jnp.concatenate(
+                    [pltpu.roll(edge_cols, 128 - at, 1), pltpu.roll(edge_cols, 64 - at, 1)], axis=0
+                )
+                above = jnp.concatenate(
+                    [pltpu.roll(edge_cols, 123 - at, 1), pltpu.roll(edge_cols, 59 - at, 1)], axis=0
+                )
+                north, south = along_y(field, below, above)
+                wind.append((east, west, north, south))
+            (ue, uw, un, us), (ve, vw, vn, vs) = wind
+            total = cum_recv[x, z] + above_cum * (0.5 * (ue - uw) + 0.5 * (vn - vs))
+            lift = jnp.clip(-lift_scale * total, -lift_limit, lift_limit)
             for f in range(3):
                 field = met[f, mine, x, z]
                 slope = half * (partner[f, x, z] - met[f, 1 - mine, x, z])
                 after = field - lift * slope
                 if f < 2:
-                    at = 2 * f + mine
-                    east, west = along_x(
-                        field,
-                        edge_send[g, pl.ds(at, 1), 0:COLS],
-                        edge_send[g, pl.ds(at + 4, 1), 0:COLS],
-                    )
-                    below = jnp.concatenate(
-                        [pltpu.roll(edge_cols, 128 - at, 1), pltpu.roll(edge_cols, 64 - at, 1)], axis=0
-                    )
-                    above = jnp.concatenate(
-                        [pltpu.roll(edge_cols, 123 - at, 1), pltpu.roll(edge_cols, 59 - at, 1)], axis=0
-                    )
-                    north, south = along_y(field, below, above)
-                    after = after + diffuse_rate * (east + west + north + south - 4.0 * field)
+                    after = after + diffuse_rate * (sum(wind[f][1:], wind[f][0]) - 4.0 * field)
                 met_out[f, mine, x, z] = after
         return 0
 
@@ -434,8 +463,9 @@
     for copy in back:
         copy.wait_recv()
     own_back.wait()
-    for copy in bulk + pairs + edges + lift_back + back:
+    for copy in pairs + edges + cum_back + back:
         copy.wait_send()
+    pl.when(near)(hand_on.wait_send)
     pl.when(grp < GRP - 1)(rows_up.wait_send)
     pl.when(grp > 0)(rows_down.wait_send)
     pl.when(gy < GY - 1)(cols_up.wait_send)
@@ -444,6 +474,17 @@
     pl.when(line > 0)(arows_down.wait_send)
     pl.when(gy < GY - 1)(acols_up.wait_send)
     pl.when(gy > 0)(acols_down.wait_send)
+
+
+def write_out(ash_ref, met_ref, ash_out, met_out, done):
+    copies = [pltpu.make_async_copy(ash_ref.at[b], ash_out.at[b], done.at[b]) for b in range(BINS)]
+    copies += [
+        pltpu.make_async_copy(met_ref.at[f], met_out.at[f], done.at[BINS + f]) for f in range(3)
+    ]
+    for copy in copies:
+        copy.start()
+    for copy in copies:
+        copy.wait()
 
 
 def body(wind_u, wind_v, theta, ash, src_x, src_y, src_rate, settle_class, settle_table):
@@ -471,7 +512,7 @@
                 pltpu.VMEM((3, NZ, ROWS, COLS), F32),
                 pltpu.VMEM((BINS, NZ, ROWS, COLS), F32),
                 pltpu.VMEM((3, NZ, ROWS, COLS), F32),
-                pltpu.VMEM((NZ, ROWS, COLS), F32),
+                pltpu.VMEM((G, ROWS, COLS), F32),
                 pltpu.VMEM((7, NZ, ROWS, COLS), F32),
                 pltpu.VMEM((NZ + 1, ROWS, COLS), F32),
                 pltpu.VMEM((NSRC, ROWS, COLS), F32),
@@ -488,7 +529,8 @@
                 dma((3, G)), dma((3, G)),
                 dma((G,)), dma((G,)),
                 dma((G,)), dma((G,)),
-                dma((G,)), dma((G,)),
+                dma((4,)), dma((2, 4)),
+                dma((1,)), dma((1,)),
                 dma((3, 4)), dma((3, 4)),
                 dma((8,)), dma((8,)),
                 dma((14,)),
@@ -504,6 +546,20 @@
                 src_x, src_y, src_rate, settle_class, settle_table,
             )
         )
+    )
+    ash_next, met_next = pl.pallas_call(
+        write_out,
+        out_shape=(
+            pltpu.HBM((BINS, NZ, ROWS, COLS), F32),
+            pltpu.HBM((3,) + tiled, F32),
+        ),
+        in_specs=[vmem, vmem],
+        out_specs=(hbm, hbm),
+        scratch_shapes=[dma((BINS + 3,))],
+        compiler_params=pltpu.CompilerParams(vmem_limit_bytes=2**20),
+    )(
+        pltpu.with_memory_space_constraint(ash_next, pltpu.VMEM),
+        pltpu.with_memory_space_constraint(met_next, pltpu.VMEM),
     )
     return ash_next, met_next.reshape(3, LV, MROWS, COLS)
 

time: 91.6 us -> 85.6 us (0.934)
  Pallas kernels: 87.8 us -> 84.3 us
  local copies, waits for them, and re-layouts: 3.16 us -> 0 us
    pallas_call x1, Pallas kernels: 87.8 us -> 81.7 us  [body(): pl.pallas_call(kernel, out_shape=(pltpu.VMEM((BINS, NZ, ROWS, COLS), F32)...]
    unnamed x2 -> x0, local copies, waits for them, and re-layouts: 3.16 us -> none
    pallas_call x0 -> x1, Pallas kernels: none -> 2.59 us  [body(): pl.pallas_call(write_out, out_shape=(pltpu.HBM((BINS, NZ, ROWS, COLS), F3...]
where the time goes in v3:
time: 85.6 us; the launch traced here: 85 us
  Pallas kernels  84.3 us (98%)
    pallas_call x1, Pallas kernels, body(): pl.pallas_call(kernel, out_shape=(pltpu.VMEM((BINS, NZ, ROWS, COLS), F32)...  81.7 us
    pallas_call x1, Pallas kernels, body(): pl.pallas_call(write_out, out_shape=(pltpu.HBM((BINS, NZ, ROWS, COLS), F3...  2.59 us

profile of v3, /device:TPU:1, one launch (start us, length us, event | category | flops | bytes accessed | tf_op | source)
XLA Modules:
  0.0 85.0 jit_solution(2703688047682849504)
XLA Ops:
  0.6 81.7 %shard_map.104 = (f32[8,32,16,256]{3,2,1,0:T(8,128)S(1)}, f32[3,2,4,4,16,256]{5,4,3,2,1,0:T(8,128)S(1)}) custom-call(f32[2,4,4,16,256]{4,3,2,1,0:T(8,128)} %bitcast.4, f32[2,4,4,16,256]{4,3,2,1,0:T(8,128)} %bitcast.5, f32[2,4,4,16,256]{4,3,2,1,0:T(8,128)} %bitcast.6, f32[8,32,16,256]{3,2,1,0:T(8,128)} %ash_ref.1, s32[16]{0:T(128)} %sx_hbm.1, s32[16]{0:T(128)} %sy_hbm.1, ...), custom_call_target="tpu_custom_call" | custom-call | tf_op jit(solution)/shard_map/pallas_call | solution.py:495
  82.4 2.6 %shard_map.105 = (f32[8,32,16,256]{3,2,1,0:T(8,128)}, f32[3,2,4,4,16,256]{5,4,3,2,1,0:T(8,128)}) custom-call(f32[8,32,16,256]{3,2,1,0:T(8,128)S(1)} %get-tuple-element.6.ash_ref, f32[3,2,4,4,16,256]{5,4,3,2,1,0:T(8,128)S(1)} %get-tuple-element.7.met_ref), custom_call_target="tpu_custom_call" | custom-call | tf_op jit(solution)/shard_map/pallas_call | solution.py:550

commit v4 on v3

--- a/solution.py
+++ b/solution.py
@@ -38,8 +38,8 @@
     sx_ref, sy_ref, rate_ref, class_ref, table_ref,
     met, partner, cum_recv, fields, conc, ret, cums, coef, dens, marks,
     row_send, row_recv, col_send, col_recv, edge_send, edge_recv,
-    arow_send, arow_recv, acol_send, acol_recv,
-    bulk_s, bulk_r, edge_s, edge_r, ret_s, ret_r, cum_s, cum_r, mate_s, mate_r, part_s, part_r, near_s, near_r, local,
+    arow_send, arow_recv, acol_send, acol_recv, tcol_send, tcol_recv,
+    bulk_s, bulk_r, edge_s, edge_r, ret_s, ret_r, cum_s, cum_r, mate_s, mate_r, part_s, part_r, near_s, near_r, local, ready,
 ):
     grp, gx, gy = lax.axis_index("grp"), lax.axis_index("gx"), lax.axis_index("gy")
     line = grp * G + gx
@@ -60,8 +60,6 @@
             )
         )
     ]
-    for copy in met_in + [ash_in] + small_in:
-        copy.start()
 
     barrier = pltpu.get_barrier_semaphore()
 
@@ -72,19 +70,27 @@
         greet((grp, jnp.bitwise_xor(gx, d), gy))
     pl.when(gy > 0)(lambda: greet((grp, gx, gy - 1)))
     pl.when(gy < GY - 1)(lambda: greet((grp, gx, gy + 1)))
-    pl.when(grp > 0)(lambda: greet((grp - 1, gx, gy)))
+    pl.when(jnp.logical_or(grp == 1, grp == 3))(lambda: greet((grp - 1, gx, gy)))
     pl.when(grp < GRP - 1)(lambda: greet((grp + 1, gx, gy)))
     far_down = jnp.logical_and(wrap_down, grp > 0)
     far_up = jnp.logical_and(wrap_up, grp < GRP - 1)
-    pl.when(far_down)(lambda: greet(row_down))
+    pl.when(jnp.logical_and(far_down, grp != 2))(lambda: greet(row_down))
     pl.when(far_up)(lambda: greet(row_up))
     count = (
         G - 1
         + (gy > 0).astype(jnp.int32) + (gy < GY - 1).astype(jnp.int32)
-        + (grp > 0).astype(jnp.int32) + (grp < GRP - 1).astype(jnp.int32)
-        + far_down.astype(jnp.int32) + far_up.astype(jnp.int32)
+        + (grp > 0).astype(jnp.int32) + (grp % 2 == 0).astype(jnp.int32)
+        + far_down.astype(jnp.int32) + jnp.logical_and(far_up, grp != 1).astype(jnp.int32)
     )
+    for copy in met_in:
+        copy.start()
     pl.semaphore_wait(barrier, count)
+
+    def tell(index, device):
+        pl.semaphore_signal(ready.at[index], inc=1, device_id=device, device_id_type=MESH)
+
+    pl.when(grp == 2)(lambda: tell(0, (grp - 1, gx, gy)))
+    pl.when(jnp.logical_and(grp == 2, wrap_down))(lambda: tell(1, row_down))
 
     def remote(src, dst, send, recv, device):
         return pltpu.make_async_remote_copy(
@@ -94,39 +100,37 @@
 
     own_levels = pl.ds(LV * gx, LV)
     own_x, own_z = gx // 4, gx % 4
+    for copy in met_in:
+        copy.wait()
     bulk = []
     for d in range(1, G):
         peer = jnp.bitwise_xor(gx, d)
-        for f in range(3):
-            copy = remote(
-                sources[f].at[:, peer // 4, peer % 4], fields.at[f, own_levels],
-                bulk_s.at[f, d], bulk_r.at[f, d], (grp, peer, gy),
-            )
-            copy.start()
-            bulk.append(copy)
-    own_bulk = []
-    for f in range(3):
-        copy = pltpu.make_async_copy(
-            sources[f].at[:, own_x, own_z], fields.at[f, own_levels], local.at[4 + f]
-        )
-        copy.start()
-        own_bulk.append(copy)
+        copy = remote(
+            met.at[:, :, peer // 4, peer % 4], fields.at[:, own_levels],
+            bulk_s.at[d], bulk_r.at[d], (grp, peer, gy),
+        )
+        copy.start()
+        bulk.append(copy)
+    own_bulk = [
+        pltpu.make_async_copy(met.at[:, :, own_x, own_z], fields.at[:, own_levels], local.at[4])
+    ]
+    own_bulk[0].start()
+    for copy in small_in + [ash_in]:
+        copy.start()
 
     mine = 1 - gx % 2
     mate = jnp.bitwise_xor(gx, 1)
     pairs = []
     for j in range(2, 4):
         group = jnp.bitwise_xor(mate % 4, j)
-        for f in range(3):
-            copy = remote(
-                sources[f].at[mine, :, group], partner.at[f, :, group],
-                part_s.at[f, j], part_r.at[f, j], (grp, mate, gy),
+        pairs.append(
+            remote(
+                met.at[:, mine, :, group], partner.at[:, :, group],
+                part_s.at[j], part_r.at[j], (grp, mate, gy),
             )
-            pairs.append(copy)
+        )
 
     lane = lax.broadcasted_iota(jnp.int32, (8, 128), 1)
-    for copy in met_in:
-        copy.wait()
     for f in range(2):
         for lev in range(LV):
             at = 2 * f + lev
@@ -163,6 +167,7 @@
 
     pl.when(gy < GY - 1)(cols_up.start)
     pl.when(gy > 0)(cols_down.start)
+    pl.when(grp == 1)(lambda: pl.semaphore_wait(ready.at[0], 1))
     pl.when(grp < GRP - 1)(rows_up.start)
     pl.when(grp > 0)(rows_down.start)
     pl.when(grp == 0)(lambda: clear(row_recv.at[0]))
@@ -198,11 +203,12 @@
     for d in range(1, G):
         peer = jnp.bitwise_xor(gx, d)
         copy = remote(
-            edge_send.at[peer], edge_recv.at[gx], edge_s.at[d], edge_r.at[d], (grp, peer, gy)
+            edge_send.at[peer, :, 0:COLS], edge_recv.at[gx],
+            edge_s.at[d], edge_r.at[d], (grp, peer, gy),
         )
         copy.start()
         edges.append(copy)
-    own_edge = pltpu.make_async_copy(edge_send.at[gx], edge_recv.at[gx], local.at[7])
+    own_edge = pltpu.make_async_copy(edge_send.at[gx, :, 0:COLS], edge_recv.at[gx], local.at[7])
     own_edge.start()
 
     row16 = lax.broadcasted_iota(jnp.int32, (ROWS, COLS), 0)
@@ -255,6 +261,7 @@
     arows_down = remote(arow_send.at[1], arow_recv.at[1], near_s.at[5], near_r.at[5], row_down)
     acols_up = remote(acol_send.at[0], acol_recv.at[0], near_s.at[6], near_r.at[6], (grp, gx, gy + 1))
     acols_down = remote(acol_send.at[1], acol_recv.at[1], near_s.at[7], near_r.at[7], (grp, gx, gy - 1))
+    pl.when(jnp.logical_and(grp == 1, wrap_up))(lambda: pl.semaphore_wait(ready.at[1], 1))
     pl.when(line < last_line)(arows_up.start)
     pl.when(line > 0)(arows_down.start)
     pl.when(gy < GY - 1)(acols_up.start)
@@ -276,6 +283,31 @@
         copy.wait()
     own_edge.wait()
 
+    def pack_tile(k, sums):
+        right, left = sums
+        for f in range(2):
+            for half in range(2):
+                at = 64 * half + NZ * f + k
+                rows = slice(8 * half, 8 * half + 8)
+                tail = pltpu.roll(fields[f, k, rows, 128:256], lax.rem(at + 1, 128), 1)
+                head = pltpu.roll(fields[f, k, rows, 0:128], at, 1)
+                right = jnp.where(lane == at, tail, right)
+                left = jnp.where(lane == at, head, left)
+        return right, left
+
+    right, left = lax.fori_loop(
+        0, NZ, pack_tile, (jnp.zeros((8, 128), F32), jnp.zeros((8, 128), F32)), unroll=4
+    )
+    tcol_send[0], tcol_send[1] = right, left
+    tcols_up = remote(tcol_send.at[0], tcol_recv.at[0], near_s.at[8], near_r.at[8], (grp, gx, gy + 1))
+    tcols_down = remote(tcol_send.at[1], tcol_recv.at[1], near_s.at[9], near_r.at[9], (grp, gx, gy - 1))
+    pl.when(gy < GY - 1)(tcols_up.start)
+    pl.when(gy > 0)(tcols_down.start)
+    pl.when(gy == 0)(lambda: clear(tcol_recv.at[0]))
+    pl.when(gy == GY - 1)(lambda: clear(tcol_recv.at[1]))
+    pl.when(gy > 0)(tcols_up.wait_recv)
+    pl.when(gy < GY - 1)(tcols_down.wait_recv)
+
     first_row, end_row = row16 == 0, row16 == ROWS - 1
     first_lane, end_lane = lane16 == 0, lane16 == COLS - 1
 
@@ -293,13 +325,13 @@
         return north, south
 
     def diagnose(g, total):
-        edge_cols = edge_recv[g, :, COLS : COLS + 128]
+        left_cols, right_cols = tcol_recv[0], tcol_recv[1]
         for lev in range(LV):
             k = LV * g + lev
             up, down = jnp.minimum(k + 1, NZ - 1), jnp.maximum(k - 1, 0)
             wind = []
             for f in range(2):
-                at = 2 * f + lev
+                at, lane_of = 2 * f + lev, NZ * f + k
                 field = fields[f, k]
                 east, west = along_x(
                     field,
@@ -307,10 +339,12 @@
                     edge_recv[g, at + 4 : at + 5, 0:COLS],
                 )
                 below = jnp.concatenate(
-                    [pltpu.roll(edge_cols, (128 - at) % 128, 1), pltpu.roll(edge_cols, 64 - at, 1)], axis=0
+                    [pltpu.roll(left_cols, lax.rem(128 - lane_of, 128), 1), pltpu.roll(left_cols, 64 - lane_of, 1)],
+                    axis=0,
                 )
                 above = jnp.concatenate(
-                    [pltpu.roll(edge_cols, 127 - at - 4, 1), pltpu.roll(edge_cols, 63 - at - 4, 1)], axis=0
+                    [pltpu.roll(right_cols, 127 - lane_of, 1), pltpu.roll(right_cols, 63 - lane_of, 1)],
+                    axis=0,
                 )
                 north, south = along_y(field, below, above)
                 slope = 0.5 * (fields[f, up] - fields[f, down])
@@ -460,12 +494,10 @@
 
     lax.fori_loop(0, 4, step_rows, 0)
 
-    for copy in back:
-        copy.wait_recv()
-    own_back.wait()
-    for copy in pairs + edges + cum_back + back:
+    for copy in pairs + edges + cum_back:
         copy.wait_send()
     pl.when(near)(hand_on.wait_send)
+    own_back.wait()
     pl.when(grp < GRP - 1)(rows_up.wait_send)
     pl.when(grp > 0)(rows_down.wait_send)
     pl.when(gy < GY - 1)(cols_up.wait_send)
@@ -474,6 +506,12 @@
     pl.when(line > 0)(arows_down.wait_send)
     pl.when(gy < GY - 1)(acols_up.wait_send)
     pl.when(gy > 0)(acols_down.wait_send)
+    pl.when(gy < GY - 1)(tcols_up.wait_send)
+    pl.when(gy > 0)(tcols_down.wait_send)
+    for copy in back:
+        copy.wait_send()
+    for copy in back:
+        copy.wait_recv()
 
 
 def write_out(ash_ref, met_ref, ash_out, met_out, done):
@@ -521,19 +559,22 @@
                 pltpu.VMEM((2, G, 8, 128), F32),
                 pltpu.VMEM((2, G, 8, 128), F32),
                 pltpu.VMEM((G, 8, COLS + 128), F32),
-                pltpu.VMEM((G, 8, COLS + 128), F32),
+                pltpu.VMEM((G, 8, COLS), F32),
                 pltpu.VMEM((2, BINS, NZ, COLS), F32),
                 pltpu.VMEM((2, BINS, NZ, COLS), F32),
                 pltpu.VMEM((2, 2, ROWS, 128), F32),
                 pltpu.VMEM((2, 2, ROWS, 128), F32),
-                dma((3, G)), dma((3, G)),
+                pltpu.VMEM((2, 8, 128), F32),
+                pltpu.VMEM((2, 8, 128), F32),
+                dma((G,)), dma((G,)),
                 dma((G,)), dma((G,)),
                 dma((G,)), dma((G,)),
                 dma((4,)), dma((2, 4)),
                 dma((1,)), dma((1,)),
-                dma((3, 4)), dma((3, 4)),
-                dma((8,)), dma((8,)),
+                dma((4,)), dma((4,)),
+                dma((10,)), dma((10,)),
                 dma((14,)),
+                pltpu.SemaphoreType.REGULAR((2,)),
             ],
             compiler_params=pltpu.CompilerParams(
                 collective_id=0, has_side_effects=True, vmem_limit_bytes=48 * 2**20

time: 85.6 us -> 83.8 us (0.979)
  Pallas kernels: 84.3 us -> 81.8 us
    pallas_call x1, Pallas kernels: 81.7 us -> 79.2 us  [body(): pl.pallas_call(kernel, out_shape=(pltpu.VMEM((BINS, NZ, ROWS, COLS), F32)...]
where the time goes in v4:
time: 83.8 us; the launch traced here: 82.4 us
  Pallas kernels  81.8 us (98%)
    pallas_call x1, Pallas kernels, body(): pl.pallas_call(kernel, out_shape=(pltpu.VMEM((BINS, NZ, ROWS, COLS), F32)...  79.2 us
    pallas_call x1, Pallas kernels, body(): pl.pallas_call(write_out, out_shape=(pltpu.HBM((BINS, NZ, ROWS, COLS), F3...  2.59 us

profile of v4, /device:TPU:1, one launch (start us, length us, event | category | flops | bytes accessed | tf_op | source)
XLA Modules:
  0.0 82.4 jit_solution(16834057751345573548)
XLA Ops:
  0.6 79.2 %shard_map.104 = (f32[8,32,16,256]{3,2,1,0:T(8,128)S(1)}, f32[3,2,4,4,16,256]{5,4,3,2,1,0:T(8,128)S(1)}) custom-call(f32[2,4,4,16,256]{4,3,2,1,0:T(8,128)} %bitcast.4, f32[2,4,4,16,256]{4,3,2,1,0:T(8,128)} %bitcast.5, f32[2,4,4,16,256]{4,3,2,1,0:T(8,128)} %bitcast.6, f32[8,32,16,256]{3,2,1,0:T(8,128)} %ash_ref.1, s32[16]{0:T(128)} %sx_hbm.1, s32[16]{0:T(128)} %sy_hbm.1, ...), custom_call_target="tpu_custom_call" | custom-call | tf_op jit(solution)/shard_map/pallas_call | solution.py:533
  79.8 2.6 %shard_map.105 = (f32[8,32,16,256]{3,2,1,0:T(8,128)}, f32[3,2,4,4,16,256]{5,4,3,2,1,0:T(8,128)}) custom-call(f32[8,32,16,256]{3,2,1,0:T(8,128)S(1)} %get-tuple-element.6.ash_ref, f32[3,2,4,4,16,256]{5,4,3,2,1,0:T(8,128)S(1)} %get-tuple-element.7.met_ref), custom_call_target="tpu_custom_call" | custom-call | tf_op jit(solution)/shard_map/pallas_call | solution.py:591

commit v5 on v4

--- a/solution.py
+++ b/solution.py
@@ -167,8 +167,7 @@
 
     pl.when(gy < GY - 1)(cols_up.start)
     pl.when(gy > 0)(cols_down.start)
-    pl.when(grp == 1)(lambda: pl.semaphore_wait(ready.at[0], 1))
-    pl.when(grp < GRP - 1)(rows_up.start)
+    pl.when(jnp.logical_and(grp < GRP - 1, grp != 1))(rows_up.start)
     pl.when(grp > 0)(rows_down.start)
     pl.when(grp == 0)(lambda: clear(row_recv.at[0]))
     pl.when(grp == GRP - 1)(lambda: clear(row_recv.at[1]))
@@ -185,6 +184,12 @@
         return 0
 
     lax.fori_loop(0, G, pack_rows, 0)
+
+    @pl.when(grp == 1)
+    def _():
+        pl.semaphore_wait(ready.at[0], 1)
+        rows_up.start()
+
     pl.when(grp > 0)(rows_up.wait_recv)
     pl.when(grp < GRP - 1)(rows_down.wait_recv)
     pl.when(gy > 0)(cols_up.wait_recv)
@@ -473,7 +478,7 @@
                     edge_send[g, pl.ds(at + 4, 1), 0:COLS],
                 )
                 below = jnp.concatenate(
-                    [pltpu.roll(edge_cols, 128 - at, 1), pltpu.roll(edge_cols, 64 - at, 1)], axis=0
+                    [pltpu.roll(edge_cols, lax.rem(128 - at, 128), 1), pltpu.roll(edge_cols, 64 - at, 1)], axis=0
                 )
                 above = jnp.concatenate(
                     [pltpu.roll(edge_cols, 123 - at, 1), pltpu.roll(edge_cols, 59 - at, 1)], axis=0
@@ -577,7 +582,7 @@
                 pltpu.SemaphoreType.REGULAR((2,)),
             ],
             compiler_params=pltpu.CompilerParams(
-                collective_id=0, has_side_effects=True, vmem_limit_bytes=48 * 2**20
+                collective_id=0, has_side_effects=True, vmem_limit_bytes=32 * 2**20
             ),
     )(
         *(

time: 83.8 us -> 83.8 us (level)
  no operation moved by 1% of the time
where the time goes in v5:
time: 83.8 us; the launch traced here: 82.4 us
  Pallas kernels  81.8 us (98%)
    pallas_call x1, Pallas kernels, body(): pl.pallas_call(kernel, out_shape=(pltpu.VMEM((BINS, NZ, ROWS, COLS), F32)...  79.2 us
    pallas_call x1, Pallas kernels, body(): pl.pallas_call(write_out, out_shape=(pltpu.HBM((BINS, NZ, ROWS, COLS), F3...  2.59 us

profile of v5, /device:TPU:1, one launch (start us, length us, event | category | flops | bytes accessed | tf_op | source)
XLA Modules:
  0.0 82.4 jit_solution(4162704193212130407)
XLA Ops:
  0.6 79.2 %shard_map.104 = (f32[8,32,16,256]{3,2,1,0:T(8,128)S(1)}, f32[3,2,4,4,16,256]{5,4,3,2,1,0:T(8,128)S(1)}) custom-call(f32[2,4,4,16,256]{4,3,2,1,0:T(8,128)} %bitcast.4, f32[2,4,4,16,256]{4,3,2,1,0:T(8,128)} %bitcast.5, f32[2,4,4,16,256]{4,3,2,1,0:T(8,128)} %bitcast.6, f32[8,32,16,256]{3,2,1,0:T(8,128)} %ash_ref.1, s32[16]{0:T(128)} %sx_hbm.1, s32[16]{0:T(128)} %sy_hbm.1, ...), custom_call_target="tpu_custom_call" | custom-call | tf_op jit(solution)/shard_map/pallas_call | solution.py:538
  79.9 2.6 %shard_map.105 = (f32[8,32,16,256]{3,2,1,0:T(8,128)}, f32[3,2,4,4,16,256]{5,4,3,2,1,0:T(8,128)}) custom-call(f32[8,32,16,256]{3,2,1,0:T(8,128)S(1)} %get-tuple-element.6.ash_ref, f32[3,2,4,4,16,256]{5,4,3,2,1,0:T(8,128)S(1)} %get-tuple-element.7.met_ref), custom_call_target="tpu_custom_call" | custom-call | tf_op jit(solution)/shard_map/pallas_call | solution.py:596
